TPU v7x, 512 devices: a whole 4x8x8 slice. The times are simulated.
512 devices in a mesh: seq: 64 (over z, y_hi, x), head: 8 (over y_lo, core).
Axes of the slice: x: 4, y: 8 (y_hi: 2, y_lo: 4; y = y_hi * 4 + y_lo), z: 8, core: 2. Of those that a mesh axis runs over, the one named last changes fastest.
Arguments:
- queries: bfloat16 [10240, 1024], P('seq', 'head'), may hold values from -15 to 15
- key_vectors: bfloat16 [10240, 1024], P('seq', 'head'), may hold values from -15 to 15
- value_vectors: bfloat16 [10240, 1024], P('seq', 'head'), may hold values from -6 to 6
- query_tangent: bfloat16 [10240, 1024], P('seq', 'head'), may hold values from -6 to 6
- key_tangent: bfloat16 [10240, 1024], P('seq', 'head'), may hold values from -6 to 6
- value_tangent: bfloat16 [10240, 1024], P('seq', 'head'), may hold values from -6 to 6
- out_weight: bfloat16 [1024, 6144], P('head'), may hold values from -0.25 to 0.25
Outputs:
- layer_out: bfloat16 [10240, 6144], P('seq', 'head')
- layer_tangent: bfloat16 [10240, 6144], P('seq', 'head')
All inputs are finite; a program needn't handle non-finite values.
Results may differ from a plain program's by a relative error of at most 0.02.
Values may be sent and summed in bfloat16 or wider, within the bound.
No kernel may reach another device: no remote copies, remote signals or barrier semaphores. Data moves between devices by JAX's collectives and lax.ppermute only.
A program may use at most 64 MiB of HBM per device.

v0:
```python
import jax
import jax.numpy as jnp
from jax import lax
from jax.sharding import PartitionSpec as P

HD = 128


def key_span(count, shard_rows):
    for factor in range(max(1, 1024 // shard_rows), 0, -1):
        if count % (factor * shard_rows) == 0:
            return factor * shard_rows
    return count


def head_scores(query_heads, key_part):
    score_scale = key_part.shape[-1] ** (-0.5)
    return (
        jnp.einsum("thd,shd->hts", query_heads, key_part, preferred_element_type=jnp.float32)
        * score_scale
    )


def tangent_scores(query_heads, qtan_heads, key_part, ktan_part):
    score_scale = key_part.shape[-1] ** (-0.5)
    both = jnp.einsum(
        "thd,shd->hts", qtan_heads, key_part, preferred_element_type=jnp.float32
    ) + jnp.einsum("thd,shd->hts", query_heads, ktan_part, preferred_element_type=jnp.float32)
    return both * score_scale


def weighted_sums(exp_weights, score_tangent, value_part, vtan_part):
    weighted = exp_weights * score_tangent
    exp_low = exp_weights.astype(jnp.bfloat16)
    weighted_low = weighted.astype(jnp.bfloat16)
    primal_add = jnp.einsum("hts,shd->htd", exp_low, value_part, preferred_element_type=jnp.float32)
    tangent_add = jnp.einsum(
        "hts,shd->htd", weighted_low, value_part, preferred_element_type=jnp.float32
    ) + jnp.einsum("hts,shd->htd", exp_low, vtan_part, preferred_element_type=jnp.float32)
    return (jnp.sum(exp_weights, axis=2), jnp.sum(weighted, axis=2), primal_add, tangent_add)


def over_spans(gathered, shard_rows, heads_here, step_fn, carried):
    count = gathered[0].shape[0]
    span_rows = key_span(count, shard_rows)

    def sub_step(block_index, inner_carry):
        key_parts = [
            lax.dynamic_slice_in_dim(member, block_index * span_rows, span_rows, 0).reshape(
                span_rows, heads_here, -1
            )
            for member in gathered
        ]
        return step_fn(inner_carry, key_parts)

    return lax.fori_loop(0, count // span_rows, sub_step, carried)


def per_device(
    queries, key_vectors, value_vectors, query_tangent, key_tangent, value_tangent, out_weight
):
    rows_here = queries.shape[0]
    heads_here = queries.shape[1] // HD
    query_heads = queries.reshape(rows_here, heads_here, HD)
    qtan_heads = query_tangent.reshape(rows_here, heads_here, HD)
    zero_rows = jnp.zeros((heads_here, rows_here), jnp.float32)
    zero_acc = jnp.zeros((heads_here, rows_here, HD), jnp.float32)
    lowest = jnp.full((heads_here, rows_here), -1e30, jnp.float32)

    def joint_step(carried, key_parts):
        run_max, run_total, run_grad, primal_acc, tangent_acc = carried
        key_part, value_part, ktan_part, vtan_part = key_parts
        scores = head_scores(query_heads, key_part)
        score_tangent = tangent_scores(query_heads, qtan_heads, key_part, ktan_part)
        new_max = jnp.maximum(run_max, jnp.max(scores, axis=2))
        decay = jnp.exp(run_max - new_max)
        exp_weights = jnp.exp(scores - new_max[..., None])
        total_add, grad_add, primal_add, tangent_add = weighted_sums(
            exp_weights, score_tangent, value_part, vtan_part
        )
        return (
            new_max,
            run_total * decay + total_add,
            run_grad * decay + grad_add,
            primal_acc * decay[..., None] + primal_add,
            tangent_acc * decay[..., None] + tangent_add,
        )

    final = over_spans(
        (
            lax.all_gather(key_vectors, "seq", axis=0, tiled=True),
            lax.all_gather(value_vectors, "seq", axis=0, tiled=True),
            lax.all_gather(key_tangent, "seq", axis=0, tiled=True),
            lax.all_gather(value_tangent, "seq", axis=0, tiled=True),
        ),
        rows_here,
        heads_here,
        joint_step,
        (lowest, zero_rows, zero_rows, zero_acc, zero_acc),
    )
    run_total, run_grad, primal_acc, tangent_acc = (final[1], final[2], final[3], final[4])
    attn_heads = primal_acc / run_total[..., None]
    tan_heads = tangent_acc / run_total[..., None] - (run_grad / run_total)[..., None] * attn_heads
    attn_out = (
        jnp.transpose(attn_heads, (1, 0, 2))
        .reshape(rows_here, heads_here * HD)
        .astype(jnp.bfloat16)
    )
    attn_tangent = (
        jnp.transpose(tan_heads, (1, 0, 2)).reshape(rows_here, heads_here * HD).astype(jnp.bfloat16)
    )
    out_part = jnp.dot(attn_out, out_weight, preferred_element_type=jnp.float32)
    tangent_part = jnp.dot(attn_tangent, out_weight, preferred_element_type=jnp.float32)
    layer_sum, tangent_sum = (
        lax.psum_scatter(
            out_part.astype(jnp.bfloat16), "head", scatter_dimension=1, tiled=True
        ).astype(jnp.float32),
        lax.psum_scatter(
            tangent_part.astype(jnp.bfloat16), "head", scatter_dimension=1, tiled=True
        ).astype(jnp.float32),
    )
    return (layer_sum.astype(jnp.bfloat16), tangent_sum.astype(jnp.bfloat16))


def solution(mesh):
    placed = (
        P("seq", "head"),
        P("seq", "head"),
        P("seq", "head"),
        P("seq", "head"),
        P("seq", "head"),
        P("seq", "head"),
        P("head", None),
    )
    return jax.shard_map(
        per_device,
        mesh=mesh,
        in_specs=placed,
        out_specs=(P("seq", "head"), P("seq", "head")),
        check_vma=False,
    )
```

profile of v0, /device:TPU:1, one launch (start us, length us, event | category | flops | bytes accessed | tf_op | source)
XLA Modules:
  0.0 786.1 jit_solution(17306325823567022550)
XLA Ops:
  10.1 142.5 %all-gather.5.cloned.1.call-done = bf16[10240,128]{1,0:T(8,128)(2,1)} async-done(((bf16[160,128]{1,0:T(8,128)(2,1)}), bf16[10240,128]{1,0:T(8,128)(2,1)}) %all-gather.5.cloned.1.call-update) | async-done | bytes 2621456 | tf_op jit(solution)/shard_map/all_gather | solution.py:91
  152.6 139.2 %all-gather.9.cloned.1.call-done = bf16[10240,128]{1,0:T(8,128)(2,1)} async-done(((bf16[160,128]{1,0:T(8,128)(2,1)}), bf16[10240,128]{1,0:T(8,128)(2,1)}) %all-gather.9.cloned.1.call-update) | async-done | bytes 2621456 | tf_op jit(solution)/shard_map/all_gather | solution.py:92
  291.8 139.2 %all-gather.7.cloned.1.call-done = bf16[10240,128]{1,0:T(8,128)(2,1)} async-done(((bf16[160,128]{1,0:T(8,128)(2,1)}), bf16[10240,128]{1,0:T(8,128)(2,1)}) %all-gather.7.cloned.1.call-update) | async-done | bytes 2621456 | tf_op jit(solution)/shard_map/all_gather | solution.py:93
  431.0 139.1 %all-gather.11.cloned.1.call-done = bf16[10240,128]{1,0:T(8,128)(2,1)} async-done(((bf16[160,128]{1,0:T(8,128)(2,1)}), bf16[10240,128]{1,0:T(8,128)(2,1)}) %all-gather.11.cloned.1.call-update) | async-done | bytes 2621456 | tf_op jit(solution)/shard_map/all_gather | solution.py:94
  570.1 120.0 %while.22 = (s32[]{:T(128)}, f32[1,160]{1,0:T(1,128)S(1)}, f32[1,160]{1,0:T(1,128)S(1)}, f32[1,160]{1,0:T(1,128)S(1)}, f32[1,160,128]{2,1,0:T(8,128)S(1)}, /*ind...) while((s32[]{:T(128)}, f32[1,160]{1,0:T(1,128)S(1)}, ...), condition=%wide.region_4.0_spmd.clone, body=%wide.region_0.0_spmd.clone.sunk | while | flops 158864480 | bytes 4889841 | solution.py:56
  571.2 1.2 fusion.67
  572.5 1.3 fusion.71
  574.0 1.2 fusion.74
  576.3 1.2 fusion.76
  578.7 1.2 fusion.67
  580.0 1.3 fusion.71
  581.5 1.2 fusion.74
  583.8 1.2 fusion.76
  586.2 1.2 fusion.67
  587.5 1.3 fusion.71
  589.0 1.2 fusion.74
  591.4 1.2 fusion.76
  593.7 1.2 fusion.67
  595.0 1.3 fusion.71
  596.5 1.2 fusion.74
  598.9 1.2 fusion.76
  601.2 1.2 fusion.67
  602.5 1.3 fusion.71
  604.0 1.2 fusion.74
  606.4 1.2 fusion.76
  608.7 1.2 fusion.67
  610.0 1.3 fusion.71
  611.5 1.2 fusion.74
  613.9 1.2 fusion.76
  616.2 1.2 fusion.67
  617.5 1.3 fusion.71
  619.0 1.2 fusion.74
  621.4 1.2 fusion.76
  623.7 1.2 fusion.67
  625.0 1.3 fusion.71
  626.5 1.2 fusion.74
  631.2 1.2 fusion.67
  632.5 1.3 fusion.71
  634.0 1.2 fusion.74
  638.7 1.2 fusion.67
  640.0 1.3 fusion.71
  641.5 1.2 fusion.74
  646.2 1.2 fusion.67
  647.5 1.3 fusion.71
  649.0 1.2 fusion.74
  653.7 1.2 fusion.67
  655.0 1.3 fusion.71
  656.5 1.2 fusion.74
  661.3 1.2 fusion.67
  662.5 1.3 fusion.71
  664.0 1.2 fusion.74
  668.8 1.2 fusion.67
  670.0 1.3 fusion.71
  671.5 1.2 fusion.74
  676.3 1.2 fusion.67
  677.5 1.3 fusion.71
  679.0 1.2 fusion.74
  683.8 1.2 fusion.67
  685.0 1.3 fusion.71
  686.6 1.2 fusion.74
  690.1 2.0 convolution_convert_fusion
  692.2 2.0 convolution_convert_fusion.1
  694.3 39.3 %reduce-scatter.5.cloned.1.call-done = bf16[160,768]{1,0:T(8,128)(2,1)} async-done(((bf16[160,6144]{1,0:T(8,128)(2,1)}), bf16[160,768]{1,0:T(8,128)(2,1)}) %reduce-scatter.5.cloned.1.call-update) | async-done | bytes 245776 | tf_op jit(solution)/shard_map/reduce_scatter | solution.py:118
  733.5 45.8 %reduce-scatter.3.cloned.1.call-done = bf16[160,768]{1,0:T(8,128)(2,1)} async-done(((bf16[160,6144]{1,0:T(8,128)(2,1)}), bf16[160,768]{1,0:T(8,128)(2,1)}) %reduce-scatter.3.cloned.1.call-update) | async-done | bytes 245776 | tf_op jit(solution)/shard_map/reduce_scatter | solution.py:115
  (141 shorter events, 54.0 us)
Async XLA Ops:
  7.2 683.0 %copy-start = (bf16[128,6144]{1,0:T(8,128)(2,1)S(1)}, bf16[128,6144]{1,0:T(8,128)(2,1)}, u32[]{:S(2)}) copy-start(bf16[128,6144]{1,0:T(8,128)(2,1)} %param.15) | copy-start | bytes 4718596
  7.2 145.4 %all-gather.5.cloned.1.call-start = ((), (), s32[]{:S(2)}) async-start(), calls=%async_computation.2 | async-start | bytes 2662400 | tf_op jit(solution)/shard_map/all_gather | solution.py:91
  7.9 283.9 %all-gather.9.cloned.1.call-start = ((), (), s32[]{:S(2)}) async-start(), calls=%async_computation.4 | async-start | bytes 2662400 | tf_op jit(solution)/shard_map/all_gather | solution.py:92
  8.7 422.3 %all-gather.7.cloned.1.call-start = ((), (), s32[]{:S(2)}) async-start(), calls=%async_computation.3 | async-start | bytes 2662400 | tf_op jit(solution)/shard_map/all_gather | solution.py:93
  9.4 560.7 %all-gather.11.cloned.1.call-start = ((), (), s32[]{:S(2)}) async-start(), calls=%async_computation.5 | async-start | bytes 2662400 | tf_op jit(solution)/shard_map/all_gather | solution.py:94
  10.0 723.5 %reduce-scatter.5.cloned.1.call-start = ((), (), s32[]{:S(2)}) async-start(), calls=%async_computation.7 | async-start | bytes 2211840 | tf_op jit(solution)/shard_map/reduce_scatter | solution.py:118
  692.2 87.1 %reduce-scatter.3.cloned.1.call-start = ((), (), s32[]{:S(2)}) async-start(), calls=%async_computation.6 | async-start | bytes 2211840 | tf_op jit(solution)/shard_map/reduce_scatter | solution.py:115
Sparse Core Ops, SparseCore 0:
  12.5 140.0 all-gather.4
  157.0 134.6 all-gather.8
  296.3 134.6 all-gather.6
  435.3 134.6 all-gather.10
  692.3 41.1 reduce-scatter.4
  737.1 42.1 reduce-scatter.2
where the time goes:
time: 790 us; the launch traced here: 786 us
  waiting for transfers between devices  648 us (82%)
  matrix products  119 us (15%)
  between operations  14.2 us (2%)
    all_gather x1, waiting for transfers between devices, per_device(): lax.all_gather(key_vectors, 'seq', axis=0, tiled=True)  142 us
    all_gather x1, waiting for transfers between devices, per_device(): lax.all_gather(key_tangent, 'seq', axis=0, tiled=True)  139 us
    all_gather x1, waiting for transfers between devices, per_device(): lax.all_gather(value_vectors, 'seq', axis=0, tiled=True)  139 us
    all_gather x1, waiting for transfers between devices, per_device(): lax.all_gather(value_tangent, 'seq', axis=0, tiled=True)  139 us
    reduce_scatter x1, waiting for transfers between devices, per_device(): lax.psum_scatter(out_part.astype(jnp.bfloat16), 'head', scatter_dimension...  45.8 us
    reduce_scatter x1, waiting for transfers between devices, per_device(): lax.psum_scatter(tangent_part.astype(jnp.bfloat16), 'head', scatter_dimen...  39.3 us
    dot_general x16, matrix products, tangent_scores(): jnp.einsum('thd,shd->hts', query_heads, ktan_part, preferred_element_type...  20.1 us
    dot_general x16, matrix products, head_scores(): jnp.einsum('thd,shd->hts', query_heads, key_part, preferred_element_type=...  19.9 us
  transfers between devices with their start and end apart: 6, of which 6 were waited for; matrix products, arithmetic and copies ran while one was open for 0% of the time, Pallas kernels for 0%

commit v1 on v0

v1 whole, which is shorter than its diff:
```python
import jax, jax.numpy as jnp
from jax import lax
from jax.sharding import PartitionSpec as P
from jax.experimental import pallas as pl
from jax.experimental.pallas import tpu as pltpu

HD = 128
SCALE = HD ** -0.5
LOG2E = 1.4426950408889634
STAT = 16
F32 = jnp.float32
BF16 = jnp.bfloat16


def dot_nt(a, b):
    return lax.dot_general(a, b, (((1,), (1,)), ((), ())), preferred_element_type=F32)


def dot_nn(a, b):
    return jnp.dot(a, b, preferred_element_type=F32)


def three_parts(value):
    high = value.astype(BF16).astype(F32)
    rest = value - high
    mid = rest.astype(BF16).astype(F32)
    return high, mid, (rest - mid)


def attention_body(nq, nk, rows, step_blocks, place_ref, *refs):
    q_refs, k_refs = refs[:nq], refs[nq:nq + nk]
    out_ref, qq, kk, vv = refs[nq + nk:]
    at = 0
    for ref in q_refs:
        for b in range(ref.shape[0]):
            span = pl.ds(at * rows, rows)
            qq[span, :HD] = ref[b, rows:]
            qq[span, HD:] = ref[b, :rows]
            at += 1
    blocks = at
    at = 0
    for ref in k_refs:
        for b in range(ref.shape[0]):
            span = pl.ds(at * rows, rows)
            kk[span, :HD] = ref[b, :rows]
            vv[span, :HD] = ref[b, rows:2 * rows]
            kk[span, HD:] = ref[b, 2 * rows:3 * rows]
            vv[span, HD:] = ref[b, 3 * rows:]
            at += 1
    span_rows = step_blocks * rows
    lane = lax.broadcasted_iota(jnp.int32, (rows, HD), 1)
    pick_row = lax.broadcasted_iota(jnp.int32, (STAT, HD), 0)
    pick_lane = lax.broadcasted_iota(jnp.int32, (STAT, HD), 1)
    pick_low = (pick_row == pick_lane).astype(F32).astype(BF16)
    pick_high = (pick_row == pick_lane + STAT // 2).astype(F32)
    pick_high = jnp.where(pick_lane < STAT // 2, pick_high, 0.0).astype(BF16)
    pick_low = jnp.where(pick_row < STAT // 2, pick_low.astype(F32), 0.0).astype(BF16)

    def step(i, carry):
        span = pl.ds(pl.multiple_of(i * span_rows, span_rows), span_rows)
        scores = dot_nt(qq[span, HD:], kk[:, :HD])
        slope = dot_nt(qq[span, :], kk[...])
        top = jnp.max(scores, axis=1, keepdims=True)
        weights = jnp.exp2((scores - top) * (SCALE * LOG2E))
        total = jnp.sum(weights, axis=1, keepdims=True)
        sloped = weights * slope
        grad = jnp.sum(sloped, axis=1, keepdims=True)
        both = dot_nn(weights.astype(BF16), vv[...])
        extra = dot_nn(sloped.astype(BF16), vv[:, :HD])
        inverse = 1.0 / total
        mean = both[:, :HD] * inverse
        slope_mean = grad * (SCALE * inverse)
        tangent = (extra * SCALE + both[:, HD:]) * inverse - slope_mean * mean
        weight_log = top * SCALE + jnp.log(total)
        stats = three_parts(weight_log) + three_parts(slope_mean)
        for b in range(step_blocks):
            part = slice(b * rows, (b + 1) * rows)
            at = place_ref[i * step_blocks + b]
            out_ref[at, :rows, :] = mean[part].astype(BF16)
            out_ref[at, rows:2 * rows, :] = tangent[part].astype(BF16)
            table = jnp.zeros((rows, HD), F32)
            for n, stat in enumerate(stats):
                table = jnp.where(lane == n, stat[part], table)
            table = jnp.concatenate([table, jnp.zeros((2 * HD - rows, HD), F32)]).astype(BF16)
            turned = dot_nt(pick_low, table[:HD]) + dot_nt(pick_high, table[HD:])
            out_ref[at, 2 * rows:, :] = turned.astype(BF16)
        return carry

    lax.fori_loop(0, blocks // step_blocks, step, 0, unroll=False)


def attention(places, q_parts, k_parts, rows, step_blocks=2):
    nblocks = sum(p.shape[0] for p in q_parts)
    nkeys = sum(p.shape[0] for p in k_parts) * rows
    body = lambda *refs: attention_body(len(q_parts), len(k_parts), rows, step_blocks, *refs)
    whole = pl.BlockSpec(memory_space=pltpu.VMEM)
    work = nblocks * rows * nkeys * HD
    return pl.pallas_call(
        body,
        out_shape=jax.ShapeDtypeStruct((nblocks, 2 * rows + STAT, HD), BF16),
        in_specs=[pl.BlockSpec(memory_space=pltpu.SMEM)] + [whole] * (len(q_parts) + len(k_parts)),
        out_specs=whole,
        scratch_shapes=[
            pltpu.VMEM((nblocks * rows, 2 * HD), BF16),
            pltpu.VMEM((nkeys, 2 * HD), BF16),
            pltpu.VMEM((nkeys, 2 * HD), BF16),
        ],
        compiler_params=pltpu.CompilerParams(vmem_limit_bytes=48 * 1024 * 1024),
        cost_estimate=pl.CostEstimate(flops=12 * work, bytes_accessed=4000000, transcendentals=work // HD),
        name="attention",
    )(places, *q_parts, *k_parts)


def merge_body(count, rows, part_ref, out_ref):
    pick_row = lax.broadcasted_iota(jnp.int32, (STAT, HD), 0)

    def pick(first, last):
        return jnp.where((pick_row >= first) & (pick_row < last), 1.0, 0.0).astype(BF16)

    def column(block, first):
        turned = lambda p: lax.dot_general(block, p, (((0,), (0,)), ((), ())), preferred_element_type=F32)
        low = turned(pick(first, first + 3))
        high = turned(pick(first + 8, first + 11))
        return jnp.concatenate([low, high[:rows - HD]])

    logs, slopes = [], []
    for b in range(count):
        block = part_ref[b, 2 * rows:, :]
        logs.append(column(block, 0))
        slopes.append(column(block, 3))
    top = logs[0]
    for b in range(1, count):
        top = jnp.maximum(top, logs[b])
    shares = [jnp.exp(one - top) for one in logs]
    total = sum(shares[1:], shares[0])
    inverse = 1.0 / total
    shares = [one * inverse for one in shares]
    slope_mean = shares[0] * slopes[0]
    for b in range(1, count):
        slope_mean += shares[b] * slopes[b]
    mean = jnp.zeros((rows, HD), F32)
    tangent = jnp.zeros((rows, HD), F32)
    for b in range(count):
        one = part_ref[b, :rows, :].astype(F32)
        mean += shares[b] * one
        tangent += shares[b] * (part_ref[b, rows:2 * rows, :].astype(F32) + (slopes[b] - slope_mean) * one)
    out_ref[:rows, :] = mean.astype(BF16)
    out_ref[rows:, :] = tangent.astype(BF16)


def merge(parts, rows):
    whole = pl.BlockSpec(memory_space=pltpu.VMEM)
    return pl.pallas_call(
        lambda *refs: merge_body(parts.shape[0], rows, *refs),
        out_shape=jax.ShapeDtypeStruct((2 * rows, HD), BF16),
        in_specs=[whole],
        out_specs=whole,
        compiler_params=pltpu.CompilerParams(vmem_limit_bytes=32 * 1024 * 1024),
        name="merge",
    )(parts)


def project_body(count, columns, core_ref, *refs):
    attn, weight = refs[:count], refs[count:2 * count]
    keep_ref, give_ref, left, right = refs[2 * count:]
    for n in range(count):
        left[:, n * HD:(n + 1) * HD] = attn[n][...]
        right[n * HD:(n + 1) * HD, :] = weight[n][...]
    core = core_ref[0]
    mine = pl.ds(pl.multiple_of(core * columns, HD), columns)
    other = pl.ds(pl.multiple_of((1 - core) * columns, HD), columns)
    give_ref[...] = dot_nn(left[...], right[:, other]).astype(BF16)
    keep_ref[...] = dot_nn(left[...], right[:, mine])


def project(core, attn, weight):
    rows, columns = attn[0].shape[0], weight[0].shape[1] // 2
    count = len(attn)
    whole = pl.BlockSpec(memory_space=pltpu.VMEM)
    return pl.pallas_call(
        lambda *refs: project_body(count, columns, *refs),
        out_shape=(
            jax.ShapeDtypeStruct((rows, columns), F32),
            jax.ShapeDtypeStruct((rows, columns), BF16),
        ),
        in_specs=[pl.BlockSpec(memory_space=pltpu.SMEM)] + [whole] * (2 * count),
        out_specs=(whole, whole),
        scratch_shapes=[
            pltpu.VMEM((rows, count * HD), BF16),
            pltpu.VMEM((count * HD, 2 * columns), BF16),
        ],
        compiler_params=pltpu.CompilerParams(vmem_limit_bytes=32 * 1024 * 1024),
        cost_estimate=pl.CostEstimate(flops=4 * rows * count * HD * columns, bytes_accessed=4000000, transcendentals=0),
        name="project",
    )(core, *attn, *weight)


def add_body(rows, keep_ref, got_ref, out_ref, tan_ref):
    out_ref[...] = (keep_ref[:rows] + got_ref[:rows].astype(F32)).astype(BF16)
    tan_ref[...] = (keep_ref[rows:] + got_ref[rows:].astype(F32)).astype(BF16)


def add_halves(keep, got):
    rows, columns = keep.shape[0] // 2, keep.shape[1]
    whole = pl.BlockSpec(memory_space=pltpu.VMEM)
    one = jax.ShapeDtypeStruct((rows, columns), BF16)
    return pl.pallas_call(
        lambda *refs: add_body(rows, *refs),
        out_shape=(one, one),
        in_specs=[whole, whole],
        out_specs=(whole, whole),
        name="add_halves",
    )(keep, got)


def turn(array, axis, count, offset):
    return lax.ppermute(array, axis, [(i, (i + offset) % count) for i in range(count)])


def per_device(queries, key_vectors, value_vectors, query_tangent, key_tangent, value_tangent, out_weight):
    rows = queries.shape[0]
    yh, x, yl, core = (lax.axis_index(name) for name in ("yh", "x", "yl", "c"))
    columns = out_weight.shape[1] // 4

    q_own = jnp.concatenate([queries, query_tangent])
    q_far = turn(q_own, "yh", 2, 1)
    k_own = jnp.concatenate([key_vectors, value_vectors, key_tangent, value_tangent])
    k_near = lax.all_gather(k_own, "zh", axis=0)
    k_pair = turn(k_near, "zl", 2, 1)
    q_pair = jnp.stack([q_own, q_far])
    q_parts = [q_pair] + [turn(q_pair, "x", 4, n) for n in (1, 2, 3)]
    w_parts = [lax.dynamic_slice_in_dim(out_weight, ((yl + n) % 4) * columns, columns, 1) for n in range(4)]
    w_parts = [w_parts[0]] + [turn(w_parts[n], "yl", 4, n) for n in (1, 2, 3)]

    row = jnp.arange(8, dtype=jnp.int32)
    places = ((x - row // 2) % 4) * 2 + jnp.where(row % 2 == 0, yh, 1 - yh)
    partial = attention(places.astype(jnp.int32), q_parts, [k_near, k_pair], rows)
    parts = lax.all_to_all(partial, ("x", "yh"), 0, 0, tiled=True)
    attn = merge(parts, rows)
    a_parts = [attn] + [turn(attn, "yl", 4, n) for n in (1, 2, 3)]
    keep, give = project(core.astype(jnp.int32).reshape(1), a_parts, w_parts)
    got = turn(give, "c", 2, 1)
    return add_halves(keep, got)


def solution(mesh):
    split = jax.sharding.Mesh(
        mesh.devices.reshape(4, 2, 2, 4, 4, 2), ("zh", "zl", "yh", "x", "yl", "c")
    )
    seq, head = ("zh", "zl", "yh", "x"), ("yl", "c")
    block = P(seq, head)
    return jax.shard_map(
        per_device,
        mesh=split,
        in_specs=(block,) * 6 + (P(head, None),),
        out_specs=(block, block),
        check_vma=False,
    )
```

time: 790 us -> 137 us (0.17)
  waiting for transfers between devices: 648 us -> 45.9 us
  matrix products: 119 us -> 0 us
  starting transfers between devices: 0.23 us -> 51.6 us
  blocking collectives: 0 us -> 22.6 us
  between operations: 14.2 us -> 0.8 us
  Pallas kernels: 0 us -> 10.6 us
    all_gather x4 -> x0, waiting for transfers between devices: 560 us -> none  [the longest x1 142 us: per_device(): lax.all_gather(key_vectors, 'seq', axis=0, tiled=True)]
    dot_general x98 -> x0, matrix products: 119 us -> none  [the longest x16 20.1 us: tangent_scores(): jnp.einsum('thd,shd->hts', query_heads, ktan_part, preferred_element_type...]
    reduce_scatter x2 -> x0, waiting for transfers between devices: 85 us -> none  [the longest x1 45.8 us: per_device(): lax.psum_scatter(out_part.astype(jnp.bfloat16), 'head', scatter_dimension...]
    ppermute x0 -> x12, starting transfers between devices: none -> 43.3 us  [turn(): lax.ppermute(array, axis, [(i, (i + offset) % count) for i in range(count)])]
    ppermute x0 -> x12, waiting for transfers between devices: none -> 37.9 us  [turn(): lax.ppermute(array, axis, [(i, (i + offset) % count) for i in range(count)])]
    all_gather x0 -> x1, blocking collectives: none -> 22.6 us  [per_device(): k_near = lax.all_gather(k_own, 'zh', axis=0)]
    pallas_call x0 -> x4, Pallas kernels: none -> 10.6 us  [the longest x1 6.89 us: attention(): pl.pallas_call(body, out_shape=jax.ShapeDtypeStruct((nblocks, 2 * rows +...]
    all_to_all x0 -> x1, starting transfers between devices: none -> 8.3 us  [per_device(): parts = lax.all_to_all(partial, ('x', 'yh'), 0, 0, tiled=True)]
  transfers between devices with their start and end apart: 6 -> 13, of which waited for: 6 -> 8; matrix products, arithmetic and copies ran while one was open for 0% -> 2% of each run, Pallas kernels for 0% -> 1%
where the time goes in v1:
time: 137 us
  starting transfers between devices  51.6 us (38%)
  waiting for transfers between devices  45.9 us (34%)
  blocking collectives  22.6 us (16%)
  Pallas kernels  10.6 us (8%)
  local copies, waits for them, and re-layouts  4.39 us (3%)
    ppermute x12, starting transfers between devices, turn(): lax.ppermute(array, axis, [(i, (i + offset) % count) for i in range(count)])  43.3 us
    ppermute x12, waiting for transfers between devices, turn(): lax.ppermute(array, axis, [(i, (i + offset) % count) for i in range(count)])  37.9 us
    all_gather x1, blocking collectives, per_device(): k_near = lax.all_gather(k_own, 'zh', axis=0)  22.6 us
    all_to_all x1, starting transfers between devices, per_device(): parts = lax.all_to_all(partial, ('x', 'yh'), 0, 0, tiled=True)  8.3 us
    all_to_all x1, waiting for transfers between devices, per_device(): parts = lax.all_to_all(partial, ('x', 'yh'), 0, 0, tiled=True)  7.97 us
    pallas_call x1, Pallas kernels, attention(): pl.pallas_call(body, out_shape=jax.ShapeDtypeStruct((nblocks, 2 * rows +...  6.89 us
  transfers between devices with their start and end apart: 13, of which 8 were waited for; matrix products, arithmetic and copies ran while one was open for 2% of the time, Pallas kernels for 1%

profile of v1, /device:TPU:1, one launch (start us, length us, event | category | flops | bytes accessed | tf_op | source)
XLA Modules:
  0.0 136.7 jit_solution(2563595937217593162)
XLA Ops:
  0.6 0.9 pad_maximum_fusion.1
  1.5 22.6 %all-gather = bf16[2560,128]{1,0:T(8,128)(2,1)S(1)} all-gather(bf16[640,128]{1,0:T(8,128)(2,1)S(1)} %pad_maximum_fusion.1), channel_id=2, replica_groups=mesh['zh'=4,'zl'=2,'yh'=2,'x'=4,'yl'=4,'c'=2] {'zh'}, dimensions={0}, use_global_device_ids=true | all-gather | bytes 819200 | tf_op jit(solution)/shard_map/all_gather | solution.py:228
  24.1 4.0 %collective-permute-start.4 = (bf16[4,640,128]{2,1,0:T(8,128)(2,1)S(1)}, bf16[4,640,128]{2,1,0:T(8,128)(2,1)S(1)}, u32[]{:S(2)}, u32[]{:S(2)}) collective-permute-start(bf16[4,640,128]{2,1,0:T(8,128)(2,1)S(1)} %bitcast.4), channel_id=1, source_target_pairs={{0,64},{64,0},{1,65},{65,1},{2,66},{66,2},{3,67},{67,3},{4,68},{68... | collective-permute-start | bytes 1966088 | tf_op jit(solution)/shard_map/ppermute | solution.py:217
  28.1 0.8 constant_dynamic-update-slice_fusion.1
  28.9 0.8 constant_dynamic-update-slice_fusion
  29.7 7.4 %collective-permute-start = (bf16[320,128]{1,0:T(8,128)(2,1)S(1)}, bf16[320,128]{1,0:T(8,128)(2,1)S(1)}, u32[]{:S(2)}, u32[]{:S(2)}) collective-permute-start(bf16[320,128]{1,0:T(8,128)(2,1)S(1)} %constant_dynamic-update-slice_fusion), channel_id=1, source_target_pairs={{0,32},{32,0},{1,33},{33,1},{2,34},{34,2},{3,35},{35,3},{4,36},{36... | collective-permute-start | bytes 245768 | tf_op jit(solution)/shard_map/ppermute | solution.py:217
  37.1 1.9 %collective-permute-done = bf16[320,128]{1,0:T(8,128)(2,1)S(1)} collective-permute-done((bf16[320,128]{1,0:T(8,128)(2,1)S(1)}, bf16[320,128]{1,0:T(8,128)(2,1)S(1)}, u32[]{:S(2)}, u32[]{:S(2)}) %collective-permute-start) | collective-permute-done | bytes 81952 | tf_op jit(solution)/shard_map/ppermute | solution.py:217
  39.1 4.4 %collective-permute-start.3 = (bf16[2,320,128]{2,1,0:T(8,128)(2,1)S(1)}, bf16[2,320,128]{2,1,0:T(8,128)(2,1)S(1)}, u32[]{:S(2)}, u32[]{:S(2)}) collective-permute-start(bf16[2,320,128]{2,1,0:T(8,128)(2,1)S(1)} %pad_maximum_fusion.refs_1_), channel_id=1, source_target_pairs={{0,24},{8,0},{16,8},{24,16},{1,25},{9,1},{17,9},{25,17},{2,26},{10... | collective-permute-start | bytes 491528 | tf_op jit(solution)/shard_map/ppermute | solution.py:217
  43.5 2.4 %collective-permute-start.2 = (bf16[2,320,128]{2,1,0:T(8,128)(2,1)S(1)}, bf16[2,320,128]{2,1,0:T(8,128)(2,1)S(1)}, u32[]{:S(2)}, u32[]{:S(2)}) collective-permute-start(bf16[2,320,128]{2,1,0:T(8,128)(2,1)S(1)} %pad_maximum_fusion.refs_1_), channel_id=1, source_target_pairs={{0,16},{8,24},{16,0},{24,8},{1,17},{9,25},{17,1},{25,9},{2,18},{10... | collective-permute-start | bytes 491528 | tf_op jit(solution)/shard_map/ppermute | solution.py:217
  45.9 2.5 %collective-permute-start.1 = (bf16[2,320,128]{2,1,0:T(8,128)(2,1)S(1)}, bf16[2,320,128]{2,1,0:T(8,128)(2,1)S(1)}, u32[]{:S(2)}, u32[]{:S(2)}) collective-permute-start(bf16[2,320,128]{2,1,0:T(8,128)(2,1)S(1)} %pad_maximum_fusion.refs_1_), channel_id=1, source_target_pairs={{0,8},{8,16},{16,24},{24,0},{1,9},{9,17},{17,25},{25,1},{2,10},{10... | collective-permute-start | bytes 491528 | tf_op jit(solution)/shard_map/ppermute | solution.py:217
  48.4 0.0 collective-permute-done.3.refs_4_
  48.4 2.6 %collective-permute-done.2.refs_3_ = bf16[2,320,128]{2,1,0:T(8,128)(2,1)S(1)} collective-permute-done((bf16[2,320,128]{2,1,0:T(8,128)(2,1)S(1)}, bf16[2,320,128]{2,1,0:T(8,128)(2,1)S(1)}, u32[]{:S(2)}, u32[]{:S(2)}) %collective-permute-start.2) | collective-permute-done | bytes 163872 | tf_op jit(solution)/shard_map/ppermute | solution.py:217
  51.0 4.0 %collective-permute-done.1.refs_2_ = bf16[2,320,128]{2,1,0:T(8,128)(2,1)S(1)} collective-permute-done((bf16[2,320,128]{2,1,0:T(8,128)(2,1)S(1)}, bf16[2,320,128]{2,1,0:T(8,128)(2,1)S(1)}, u32[]{:S(2)}, u32[]{:S(2)}) %collective-permute-start.1) | collective-permute-done | bytes 163872 | tf_op jit(solution)/shard_map/ppermute | solution.py:217
  55.0 0.0 collective-permute-done.4.refs_6_
  55.0 0.0 copy-start.1
  55.1 6.9 %attention.1 = bf16[8,336,128]{2,1,0:T(8,128)(2,1)} custom-call(s32[8]{0:T(128)S(1)} %fusion.refs_0_, bf16[2,320,128]{2,1,0:T(8,128)(2,1)S(1)} %pad_maximum_fusion.refs_1_, bf16[2,320,128]{2,1,0:T(8,128)(2,1)S(1)} %collective-permute-done.1.refs_2_, bf16[2,320,128]{2,1,0:T(8,128)(2,1)S(1)} %collective-permute-done.2.refs_3_, ...), custom_call_target="tpu_custom_call" | custom-call | flops 2516582400 | bytes 4000000 | tf_op jit(solution)/shard_map/attention/pallas_call | solution.py:98
  61.9 8.3 %all-to-all-start = ((bf16[8,336,128]{2,1,0:T(8,128)(2,1)}), bf16[8,336,128]{2,1,0:T(8,128)(2,1)S(1)}, u32[]{:S(2)}, u32[]{:S(2)}) async-start(bf16[8,336,128]{2,1,0:T(8,128)(2,1)} %attention.1), calls=%async_computation | async-start | bytes 1376256 | tf_op jit(solution)/shard_map/all_to_all | solution.py:238
  70.2 0.0 copy-done.1
  70.2 1.1 constant_dynamic-slice_fusion
  71.3 2.9 %collective-permute-start.10 = (bf16[128,1536]{1,0:T(8,128)(2,1)}, bf16[128,1536]{1,0:T(8,128)(2,1)S(1)}, u32[]{:S(2)}, u32[]{:S(2)}) collective-permute-start(bf16[128,1536]{1,0:T(8,128)(2,1)} %get-tuple-element.6), channel_id=1, source_target_pairs={{0,6},{2,0},{4,2},{6,4},{1,7},{3,1},{5,3},{7,5},{8,14},{10,8},{12,... | collective-permute-start | bytes 1179656 | tf_op jit(solution)/shard_map/ppermute | solution.py:217
  74.2 2.4 %collective-permute-start.8 = (bf16[128,1536]{1,0:T(8,128)(2,1)}, bf16[128,1536]{1,0:T(8,128)(2,1)S(1)}, u32[]{:S(2)}, u32[]{:S(2)}) collective-permute-start(bf16[128,1536]{1,0:T(8,128)(2,1)} %get-tuple-element.7), channel_id=1, source_target_pairs={{0,2},{2,4},{4,6},{6,0},{1,3},{3,5},{5,7},{7,1},{8,10},{10,12},{12... | collective-permute-start | bytes 1179656 | tf_op jit(solution)/shard_map/ppermute | solution.py:217
  76.6 1.9 %collective-permute-start.9 = (bf16[128,1536]{1,0:T(8,128)(2,1)}, bf16[128,1536]{1,0:T(8,128)(2,1)S(1)}, u32[]{:S(2)}, u32[]{:S(2)}) collective-permute-start(bf16[128,1536]{1,0:T(8,128)(2,1)} %get-tuple-element.9), channel_id=1, source_target_pairs={{0,4},{2,6},{4,0},{6,2},{1,5},{3,7},{5,1},{7,3},{8,12},{10,14},{12... | collective-permute-start | bytes 1179656 | tf_op jit(solution)/shard_map/ppermute | solution.py:217
  78.5 8.0 %all-to-all-done.refs_0_ = bf16[8,336,128]{2,1,0:T(8,128)(2,1)S(1)} async-done(((bf16[8,336,128]{2,1,0:T(8,128)(2,1)}), bf16[8,336,128]{2,1,0:T(8,128)(2,1)S(1)}, u32[]{:S(2)}, u32[]{:S(2)}) %all-to-all-start) | async-done | bytes 688160 | tf_op jit(solution)/shard_map/all_to_all | solution.py:238
  86.5 0.8 merge.1.refs_1_
  87.3 1.9 %collective-permute-start.7 = (bf16[320,128]{1,0:T(8,128)(2,1)S(1)}, bf16[320,128]{1,0:T(8,128)(2,1)S(1)}, u32[]{:S(2)}, u32[]{:S(2)}) collective-permute-start(bf16[320,128]{1,0:T(8,128)(2,1)S(1)} %merge.1.refs_1_), channel_id=1, source_target_pairs={{0,6},{2,0},{4,2},{6,4},{1,7},{3,1},{5,3},{7,5},{8,14},{10,8},{12,... | collective-permute-start | bytes 245768 | tf_op jit(solution)/shard_map/ppermute | solution.py:217
  89.2 6.7 %collective-permute-start.6 = (bf16[320,128]{1,0:T(8,128)(2,1)S(1)}, bf16[320,128]{1,0:T(8,128)(2,1)S(1)}, u32[]{:S(2)}, u32[]{:S(2)}) collective-permute-start(bf16[320,128]{1,0:T(8,128)(2,1)S(1)} %merge.1.refs_1_), channel_id=1, source_target_pairs={{0,4},{2,6},{4,0},{6,2},{1,5},{3,7},{5,1},{7,3},{8,12},{10,14},{12... | collective-permute-start | bytes 245768 | tf_op jit(solution)/shard_map/ppermute | solution.py:217
  95.9 0.0 collective-permute-done.10.refs_8_
  95.9 4.1 %collective-permute-start.5 = (bf16[320,128]{1,0:T(8,128)(2,1)S(1)}, bf16[320,128]{1,0:T(8,128)(2,1)S(1)}, u32[]{:S(2)}, u32[]{:S(2)}) collective-permute-start(bf16[320,128]{1,0:T(8,128)(2,1)S(1)} %merge.1.refs_1_), channel_id=1, source_target_pairs={{0,2},{2,4},{4,6},{6,0},{1,3},{3,5},{5,7},{7,1},{8,10},{10,12},{12... | collective-permute-start | bytes 245768 | tf_op jit(solution)/shard_map/ppermute | solution.py:217
  100.0 1.9 %collective-permute-done.8.refs_6_ = bf16[128,1536]{1,0:T(8,128)(2,1)S(1)} collective-permute-done((bf16[128,1536]{1,0:T(8,128)(2,1)}, bf16[128,1536]{1,0:T(8,128)(2,1)S(1)}, u32[]{:S(2)}, u32[]{:S(2)}) %collective-permute-start.8) | collective-permute-done | bytes 393248 | tf_op jit(solution)/shard_map/ppermute | solution.py:217
  101.9 22.5 %collective-permute-done.9.refs_7_ = bf16[128,1536]{1,0:T(8,128)(2,1)S(1)} collective-permute-done((bf16[128,1536]{1,0:T(8,128)(2,1)}, bf16[128,1536]{1,0:T(8,128)(2,1)S(1)}, u32[]{:S(2)}, u32[]{:S(2)}) %collective-permute-start.9) | collective-permute-done | bytes 393248 | tf_op jit(solution)/shard_map/ppermute | solution.py:217
  124.4 0.0 collective-permute-done.7.refs_4_
  124.4 3.5 %collective-permute-done.6.refs_3_ = bf16[320,128]{1,0:T(8,128)(2,1)S(1)} collective-permute-done((bf16[320,128]{1,0:T(8,128)(2,1)S(1)}, bf16[320,128]{1,0:T(8,128)(2,1)S(1)}, u32[]{:S(2)}, u32[]{:S(2)}) %collective-permute-start.6) | collective-permute-done | bytes 81952 | tf_op jit(solution)/shard_map/ppermute | solution.py:217
  127.9 0.0 collective-permute-done.5.refs_2_
  127.9 0.8 project.1
  128.7 0.0 copy-start
  128.7 1.0 copy-done
  129.7 2.6 %collective-permute-start.11 = (bf16[320,768]{1,0:T(8,128)(2,1)S(1)}, bf16[320,768]{1,0:T(8,128)(2,1)S(1)}, u32[]{:S(2)}, u32[]{:S(2)}) collective-permute-start(bf16[320,768]{1,0:T(8,128)(2,1)S(1)} %get-tuple-element.5), channel_id=1, source_target_pairs={{0,1},{1,0},{2,3},{3,2},{4,5},{5,4},{6,7},{7,6},{8,9},{9,8},{10,11... | collective-permute-start | bytes 1474568 | tf_op jit(solution)/shard_map/ppermute | solution.py:217
  132.3 1.5 %collective-permute-done.11.refs_1_ = bf16[320,768]{1,0:T(8,128)(2,1)S(1)} collective-permute-done((bf16[320,768]{1,0:T(8,128)(2,1)S(1)}, bf16[320,768]{1,0:T(8,128)(2,1)S(1)}, u32[]{:S(2)}, u32[]{:S(2)}) %collective-permute-start.11) | collective-permute-done | bytes 491552 | tf_op jit(solution)/shard_map/ppermute | solution.py:217
  133.8 0.0 copy-start.2
  133.8 0.8 copy-done.2
  134.6 2.1 %add_halves.1 = (bf16[160,768]{1,0:T(8,128)(2,1)}, bf16[160,768]{1,0:T(8,128)(2,1)}) custom-call(f32[320,768]{1,0:T(8,128)} %copy-done, bf16[320,768]{1,0:T(8,128)(2,1)} %copy-done.2), custom_call_target="tpu_custom_call" | custom-call | tf_op jit(solution)/shard_map/add_halves/pallas_call | solution.py:207
  (2 shorter events, 0.0 us)
Async XLA Ops:
  24.1 30.9 %collective-permute-start.4 = (bf16[4,640,128]{2,1,0:T(8,128)(2,1)S(1)}, bf16[4,640,128]{2,1,0:T(8,128)(2,1)S(1)}, u32[]{:S(2)}, u32[]{:S(2)}) collective-permute-start(bf16[4,640,128]{2,1,0:T(8,128)(2,1)S(1)} %bitcast.4), channel_id=1, source_target_pairs={{0,64},{64,0},{1,65},{65,1},{2,66},{66,2},{3,67},{67,3},{4,68},{68... | collective-permute-start | bytes 1966088 | tf_op jit(solution)/shard_map/ppermute | solution.py:217
  29.7 9.4 %collective-permute-start = (bf16[320,128]{1,0:T(8,128)(2,1)S(1)}, bf16[320,128]{1,0:T(8,128)(2,1)S(1)}, u32[]{:S(2)}, u32[]{:S(2)}) collective-permute-start(bf16[320,128]{1,0:T(8,128)(2,1)S(1)} %constant_dynamic-update-slice_fusion), channel_id=1, source_target_pairs={{0,32},{32,0},{1,33},{33,1},{2,34},{34,2},{3,35},{35,3},{4,36},{36... | collective-permute-start | bytes 245768 | tf_op jit(solution)/shard_map/ppermute | solution.py:217
  39.1 9.4 %collective-permute-start.3 = (bf16[2,320,128]{2,1,0:T(8,128)(2,1)S(1)}, bf16[2,320,128]{2,1,0:T(8,128)(2,1)S(1)}, u32[]{:S(2)}, u32[]{:S(2)}) collective-permute-start(bf16[2,320,128]{2,1,0:T(8,128)(2,1)S(1)} %pad_maximum_fusion.refs_1_), channel_id=1, source_target_pairs={{0,24},{8,0},{16,8},{24,16},{1,25},{9,1},{17,9},{25,17},{2,26},{10... | collective-permute-start | bytes 491528 | tf_op jit(solution)/shard_map/ppermute | solution.py:217
  43.5 7.6 %collective-permute-start.2 = (bf16[2,320,128]{2,1,0:T(8,128)(2,1)S(1)}, bf16[2,320,128]{2,1,0:T(8,128)(2,1)S(1)}, u32[]{:S(2)}, u32[]{:S(2)}) collective-permute-start(bf16[2,320,128]{2,1,0:T(8,128)(2,1)S(1)} %pad_maximum_fusion.refs_1_), channel_id=1, source_target_pairs={{0,16},{8,24},{16,0},{24,8},{1,17},{9,25},{17,1},{25,9},{2,18},{10... | collective-permute-start | bytes 491528 | tf_op jit(solution)/shard_map/ppermute | solution.py:217
  45.9 9.2 %collective-permute-start.1 = (bf16[2,320,128]{2,1,0:T(8,128)(2,1)S(1)}, bf16[2,320,128]{2,1,0:T(8,128)(2,1)S(1)}, u32[]{:S(2)}, u32[]{:S(2)}) collective-permute-start(bf16[2,320,128]{2,1,0:T(8,128)(2,1)S(1)} %pad_maximum_fusion.refs_1_), channel_id=1, source_target_pairs={{0,8},{8,16},{16,24},{24,0},{1,9},{9,17},{17,25},{25,1},{2,10},{10... | collective-permute-start | bytes 491528 | tf_op jit(solution)/shard_map/ppermute | solution.py:217
  55.0 15.2 %copy-start.1 = (bf16[128,6144]{1,0:T(8,128)(2,1)S(1)}, bf16[128,6144]{1,0:T(8,128)(2,1)}, u32[]{:S(2)}) copy-start(bf16[128,6144]{1,0:T(8,128)(2,1)} %param.13) | copy-start | bytes 4718596
  61.9 24.5 %all-to-all-start = ((bf16[8,336,128]{2,1,0:T(8,128)(2,1)}), bf16[8,336,128]{2,1,0:T(8,128)(2,1)S(1)}, u32[]{:S(2)}, u32[]{:S(2)}) async-start(bf16[8,336,128]{2,1,0:T(8,128)(2,1)} %attention.1), calls=%async_computation | async-start | bytes 1376256 | tf_op jit(solution)/shard_map/all_to_all | solution.py:238
  71.3 24.6 %collective-permute-start.10 = (bf16[128,1536]{1,0:T(8,128)(2,1)}, bf16[128,1536]{1,0:T(8,128)(2,1)S(1)}, u32[]{:S(2)}, u32[]{:S(2)}) collective-permute-start(bf16[128,1536]{1,0:T(8,128)(2,1)} %get-tuple-element.6), channel_id=1, source_target_pairs={{0,6},{2,0},{4,2},{6,4},{1,7},{3,1},{5,3},{7,5},{8,14},{10,8},{12,... | collective-permute-start | bytes 1179656 | tf_op jit(solution)/shard_map/ppermute | solution.py:217
  74.2 27.7 %collective-permute-start.8 = (bf16[128,1536]{1,0:T(8,128)(2,1)}, bf16[128,1536]{1,0:T(8,128)(2,1)S(1)}, u32[]{:S(2)}, u32[]{:S(2)}) collective-permute-start(bf16[128,1536]{1,0:T(8,128)(2,1)} %get-tuple-element.7), channel_id=1, source_target_pairs={{0,2},{2,4},{4,6},{6,0},{1,3},{3,5},{5,7},{7,1},{8,10},{10,12},{12... | collective-permute-start | bytes 1179656 | tf_op jit(solution)/shard_map/ppermute | solution.py:217
  76.6 47.8 %collective-permute-start.9 = (bf16[128,1536]{1,0:T(8,128)(2,1)}, bf16[128,1536]{1,0:T(8,128)(2,1)S(1)}, u32[]{:S(2)}, u32[]{:S(2)}) collective-permute-start(bf16[128,1536]{1,0:T(8,128)(2,1)} %get-tuple-element.9), channel_id=1, source_target_pairs={{0,4},{2,6},{4,0},{6,2},{1,5},{3,7},{5,1},{7,3},{8,12},{10,14},{12... | collective-permute-start | bytes 1179656 | tf_op jit(solution)/shard_map/ppermute | solution.py:217
  87.3 37.2 %collective-permute-start.7 = (bf16[320,128]{1,0:T(8,128)(2,1)S(1)}, bf16[320,128]{1,0:T(8,128)(2,1)S(1)}, u32[]{:S(2)}, u32[]{:S(2)}) collective-permute-start(bf16[320,128]{1,0:T(8,128)(2,1)S(1)} %merge.1.refs_1_), channel_id=1, source_target_pairs={{0,6},{2,0},{4,2},{6,4},{1,7},{3,1},{5,3},{7,5},{8,14},{10,8},{12,... | collective-permute-start | bytes 245768 | tf_op jit(solution)/shard_map/ppermute | solution.py:217
  89.2 38.7 %collective-permute-start.6 = (bf16[320,128]{1,0:T(8,128)(2,1)S(1)}, bf16[320,128]{1,0:T(8,128)(2,1)S(1)}, u32[]{:S(2)}, u32[]{:S(2)}) collective-permute-start(bf16[320,128]{1,0:T(8,128)(2,1)S(1)} %merge.1.refs_1_), channel_id=1, source_target_pairs={{0,4},{2,6},{4,0},{6,2},{1,5},{3,7},{5,1},{7,3},{8,12},{10,14},{12... | collective-permute-start | bytes 245768 | tf_op jit(solution)/shard_map/ppermute | solution.py:217
  95.9 32.0 %collective-permute-start.5 = (bf16[320,128]{1,0:T(8,128)(2,1)S(1)}, bf16[320,128]{1,0:T(8,128)(2,1)S(1)}, u32[]{:S(2)}, u32[]{:S(2)}) collective-permute-start(bf16[320,128]{1,0:T(8,128)(2,1)S(1)} %merge.1.refs_1_), channel_id=1, source_target_pairs={{0,2},{2,4},{4,6},{6,0},{1,3},{3,5},{5,7},{7,1},{8,10},{10,12},{12... | collective-permute-start | bytes 245768 | tf_op jit(solution)/shard_map/ppermute | solution.py:217
  128.7 1.0 copy-start
  129.7 4.1 %collective-permute-start.11 = (bf16[320,768]{1,0:T(8,128)(2,1)S(1)}, bf16[320,768]{1,0:T(8,128)(2,1)S(1)}, u32[]{:S(2)}, u32[]{:S(2)}) collective-permute-start(bf16[320,768]{1,0:T(8,128)(2,1)S(1)} %get-tuple-element.5), channel_id=1, source_target_pairs={{0,1},{1,0},{2,3},{3,2},{4,5},{5,4},{6,7},{7,6},{8,9},{9,8},{10,11... | collective-permute-start | bytes 1474568 | tf_op jit(solution)/shard_map/ppermute | solution.py:217
  133.8 0.8 copy-start.2

commit v2 on v1

v2 whole, which is shorter than its diff:
```python
import jax, jax.numpy as jnp
from jax import lax
from jax.sharding import PartitionSpec as P
from jax.experimental import pallas as pl
from jax.experimental.pallas import tpu as pltpu

HD = 128
SCALE = HD ** -0.5
LOG2E = 1.4426950408889634
STAT = 16
F32 = jnp.float32
BF16 = jnp.bfloat16


def dot_nt(a, b):
    return lax.dot_general(a, b, (((1,), (1,)), ((), ())), preferred_element_type=F32)


def dot_nn(a, b):
    return jnp.dot(a, b, preferred_element_type=F32)


def three_parts(value):
    high = value.astype(BF16).astype(F32)
    rest = value - high
    mid = rest.astype(BF16).astype(F32)
    return high, mid, (rest - mid)


WHOLE = pl.BlockSpec(memory_space=pltpu.VMEM)
SCALAR = pl.BlockSpec(memory_space=pltpu.SMEM)


def limit(mib):
    return pltpu.CompilerParams(vmem_limit_bytes=mib * 1024 * 1024)


def stat_rows(stats, rows):
    lane = lax.broadcasted_iota(jnp.int32, (rows, HD), 1)
    pick_row = lax.broadcasted_iota(jnp.int32, (STAT, HD), 0)
    pick_lane = lax.broadcasted_iota(jnp.int32, (STAT, HD), 1)
    half = STAT // 2
    low = jnp.where((pick_row == pick_lane) & (pick_row < half), 1.0, 0.0).astype(BF16)
    high = jnp.where((pick_row == pick_lane + half) & (pick_lane < half), 1.0, 0.0).astype(BF16)
    table = jnp.zeros((rows, HD), F32)
    for n, stat in enumerate(stats):
        table = jnp.where(lane == n, stat, table)
    table = jnp.concatenate([table, jnp.zeros((2 * HD - rows, HD), F32)]).astype(BF16)
    return (dot_nt(low, table[:HD]) + dot_nt(high, table[HD:])).astype(BF16)


def stat_columns(block, rows, first):
    pick_row = lax.broadcasted_iota(jnp.int32, (STAT, HD), 0)

    def turned(at):
        pick = jnp.where((pick_row >= at) & (pick_row < at + 3), 1.0, 0.0).astype(BF16)
        return lax.dot_general(block, pick, (((0,), (0,)), ((), ())), preferred_element_type=F32)

    return jnp.concatenate([turned(first), turned(first + STAT // 2)[: rows - HD]])


def attention_tile(q_ref, kk, vv, span):
    scores = dot_nt(q_ref[span, HD:], kk[:, :HD])
    slope = dot_nt(q_ref[span, :], kk[...])
    top = jnp.max(scores, axis=1, keepdims=True)
    weights = jnp.exp2((scores - top) * (SCALE * LOG2E))
    total = jnp.sum(weights, axis=1, keepdims=True)
    sloped = weights * slope
    grad = jnp.sum(sloped, axis=1, keepdims=True)
    both = dot_nn(weights.astype(BF16), vv[...])
    extra = dot_nn(sloped.astype(BF16), vv[:, :HD])
    inverse = 1.0 / total
    mean = both[:, :HD] * inverse
    slope_mean = grad * (SCALE * inverse)
    tangent = (extra * SCALE + both[:, HD:]) * inverse - slope_mean * mean
    return mean, tangent, top * SCALE + jnp.log(total), slope_mean


def attention_body(rows, step_blocks, place_ref, qa_ref, qb_ref, ka_ref, kb_ref, out_ref, qq, kk, vv):
    at = 0
    for q_ref in (qa_ref, qb_ref):
        for b in range(q_ref.shape[0]):
            span = pl.ds(at * rows, rows)
            qq[span, :HD] = q_ref[b, rows:]
            qq[span, HD:] = q_ref[b, :rows]
            at += 1
    blocks, at = at, 0
    for k_ref in (ka_ref, kb_ref):
        for b in range(k_ref.shape[0]):
            span = pl.ds(at * rows, rows)
            kk[span, :HD] = k_ref[b, :rows]
            vv[span, :HD] = k_ref[b, rows:2 * rows]
            kk[span, HD:] = k_ref[b, 2 * rows:3 * rows]
            vv[span, HD:] = k_ref[b, 3 * rows:]
            at += 1
    span_rows = step_blocks * rows

    def step(i, carry):
        span = pl.ds(pl.multiple_of(i * span_rows, span_rows), span_rows)
        mean, tangent, log, slope = attention_tile(qq, kk, vv, span)
        stats = three_parts(log) + three_parts(slope)
        for b in range(step_blocks):
            part = slice(b * rows, (b + 1) * rows)
            at = place_ref[i * step_blocks + b]
            out_ref[at, :rows, :] = mean[part].astype(BF16)
            out_ref[at, rows:2 * rows, :] = tangent[part].astype(BF16)
            out_ref[at, 2 * rows:, :] = stat_rows([s[part] for s in stats], rows)
        return carry

    lax.fori_loop(0, blocks // step_blocks, step, 0)


def attention(places, queries, keys, rows, step_blocks=4):
    blocks, nkeys = (sum(p.shape[0] for p in parts) for parts in (queries, keys))
    nkeys *= rows
    work = blocks * rows * nkeys * HD
    return pl.pallas_call(
        lambda *refs: attention_body(rows, step_blocks, *refs),
        out_shape=jax.ShapeDtypeStruct((blocks, 2 * rows + STAT, HD), BF16),
        in_specs=[SCALAR] + [WHOLE] * 4,
        out_specs=WHOLE,
        scratch_shapes=[
            pltpu.VMEM((blocks * rows, 2 * HD), BF16),
            pltpu.VMEM((nkeys, 2 * HD), BF16),
            pltpu.VMEM((nkeys, 2 * HD), BF16),
        ],
        compiler_params=limit(32),
        cost_estimate=pl.CostEstimate(flops=12 * work, bytes_accessed=4000000, transcendentals=work // HD),
        name="attention",
    )(places, *queries, *keys)


def merged(blocks, rows):
    logs = [stat_columns(block[2 * rows:, :], rows, 0) for block in blocks]
    slopes = [stat_columns(block[2 * rows:, :], rows, 3) for block in blocks]
    top = logs[0]
    for log in logs[1:]:
        top = jnp.maximum(top, log)
    shares = [jnp.exp(log - top) for log in logs]
    total = sum(shares[1:], shares[0])
    inverse = 1.0 / total
    slope_mean = sum([s * g for s, g in zip(shares[1:], slopes[1:])], shares[0] * slopes[0]) * inverse
    mean = jnp.zeros((rows, HD), F32)
    tangent = jnp.zeros((rows, HD), F32)
    for block, share, slope in zip(blocks, shares, slopes):
        one = block[:rows, :].astype(F32)
        mean += share * one
        tangent += share * (block[rows:2 * rows, :].astype(F32) + (slope - slope_mean) * one)
    return mean * inverse, tangent * inverse, top + jnp.log(total), slope_mean


def merge_body(rows, copies, part_ref, out_ref):
    mean, tangent, _, _ = merged([part_ref[b] for b in range(part_ref.shape[0])], rows)
    for n in range(copies):
        out_ref[n, :rows, :] = mean.astype(BF16)
        out_ref[n, rows:, :] = tangent.astype(BF16)


def merge(parts, rows, copies):
    return pl.pallas_call(
        lambda *refs: merge_body(rows, copies, *refs),
        out_shape=jax.ShapeDtypeStruct((copies, 2 * rows, HD), BF16),
        in_specs=[WHOLE],
        out_specs=WHOLE,
        compiler_params=limit(12),
        name="merge",
    )(parts)


def project_body(count, columns, at_ref, attn_ref, own_ref, *refs):
    here, there = refs[:count - 1], refs[count - 1]
    keep_ref, give_ref, left, right = refs[count:]
    core, half, part = at_ref[0], at_ref[1], HD // 2
    right[:HD, :] = own_ref[...]
    for n in range(count):
        left[:, n * HD:(n + 1) * HD] = attn_ref[at_ref[2 + n]]
        if n:
            right[pl.ds(pl.multiple_of(n * HD + half * part, part), part), :] = here[n - 1][...]
            right[pl.ds(pl.multiple_of(n * HD + (1 - half) * part, part), part), :] = there[n - 1]
    mine = pl.ds(pl.multiple_of(core * columns, HD), columns)
    other = pl.ds(pl.multiple_of((1 - core) * columns, HD), columns)
    give_ref[...] = dot_nn(left[...], right[:, other]).astype(BF16)
    keep_ref[...] = dot_nn(left[...], right[:, mine])


def project(places, attn, own, here, there):
    rows, columns, count = attn.shape[1], own.shape[1] // 2, attn.shape[0]
    return pl.pallas_call(
        lambda *refs: project_body(count, columns, *refs),
        out_shape=(
            jax.ShapeDtypeStruct((rows, columns), F32),
            jax.ShapeDtypeStruct((rows, columns), BF16),
        ),
        in_specs=[SCALAR] + [WHOLE] * (2 + count),
        out_specs=(WHOLE, WHOLE),
        scratch_shapes=[
            pltpu.VMEM((rows, count * HD), BF16),
            pltpu.VMEM((count * HD, 2 * columns), BF16),
        ],
        compiler_params=limit(12),
        cost_estimate=pl.CostEstimate(flops=4 * rows * count * HD * columns, bytes_accessed=4000000, transcendentals=0),
        name="project",
    )(places, attn, own, *here, there)


def add_body(rows, keep_ref, got_ref, out_ref, tan_ref):
    out_ref[...] = (keep_ref[:rows] + got_ref[:rows].astype(F32)).astype(BF16)
    tan_ref[...] = (keep_ref[rows:] + got_ref[rows:].astype(F32)).astype(BF16)


def add_halves(keep, got):
    rows, columns = keep.shape[0] // 2, keep.shape[1]
    one = jax.ShapeDtypeStruct((rows, columns), BF16)
    return pl.pallas_call(
        lambda *refs: add_body(rows, *refs),
        out_shape=(one, one),
        in_specs=[WHOLE, WHOLE],
        out_specs=(WHOLE, WHOLE),
        compiler_params=limit(4),
        name="add_halves",
    )(keep, got)


def prepare_body(rows, copies, q_ref, k_ref, v_ref, qt_ref, kt_ref, vt_ref, queries_ref, keys_ref, spread_ref):
    queries_ref[:rows, :] = q_ref[...]
    queries_ref[rows:, :] = qt_ref[...]
    for n, ref in enumerate((k_ref, v_ref, kt_ref, vt_ref)):
        span = pl.ds(n * rows, rows)
        value = ref[...]
        keys_ref[span, :] = value
        for m in range(copies):
            spread_ref[m, span, :] = value


def prepare(arrays, copies):
    rows = arrays[0].shape[0]
    return pl.pallas_call(
        lambda *refs: prepare_body(rows, copies, *refs),
        out_shape=(
            jax.ShapeDtypeStruct((2 * rows, HD), BF16),
            jax.ShapeDtypeStruct((4 * rows, HD), BF16),
            jax.ShapeDtypeStruct((copies, 4 * rows, HD), BF16),
        ),
        grid=(1,),
        in_specs=[pl.BlockSpec((rows, HD), lambda i: (0, 0))] * 6,
        out_specs=(WHOLE,) * 3,
        compiler_params=limit(56),
        name="prepare",
    )(*arrays)


def turn(array, axis, count, offset):
    return lax.ppermute(array, axis, [(i, (i + offset) % count) for i in range(count)])


def spread(array, axis, count):
    return lax.all_to_all(jnp.broadcast_to(array[None], (count,) + array.shape), axis, 0, 0, tiled=True)


def per_device(queries, key_vectors, value_vectors, query_tangent, key_tangent, value_tangent, out_weight):
    rows = queries.shape[0]
    yl, zl, core = lax.axis_index("yl"), lax.axis_index("zl"), lax.axis_index("c")
    columns = out_weight.shape[1] // 4

    arrays = (queries, key_vectors, value_vectors, query_tangent, key_tangent, value_tangent)
    q_own, k_own, k_spread = prepare(arrays, 4)
    k_first = lax.all_to_all(k_spread, "zh", 0, 0, tiled=True)
    k_far = turn(k_own, "yh", 2, 1)
    q_near = lax.all_gather(q_own, "x", axis=0)
    q_near, k_first, k_far = lax.optimization_barrier((q_near, k_first, k_far))
    k_second = spread(k_far, "zh", 4)
    q_pair = turn(q_near, "zl", 2, 1)

    def weight_of(n, first, height):
        at = (first, ((yl + n) % 4) * columns)
        return lax.dynamic_slice(out_weight, at, (height, columns))

    w_own = weight_of(0, 0, HD)
    w_here = [turn(weight_of(n, zl * (HD // 2), HD // 2), "yl", 4, n) for n in (1, 2, 3)]

    block = jnp.arange(8)
    spots = ((block % 4) * 2 + jnp.where(block < 4, zl, 1 - zl)).astype(jnp.int32)
    partial = attention(spots, (q_near, q_pair), (k_first, k_second), rows)
    partial, w_here = lax.optimization_barrier((partial, w_here))
    parts = lax.all_to_all(partial, ("x", "zl"), 0, 0, tiled=True)
    near = [(z, (z + 1) % 8 if z % 2 else (z - 1) % 8) for z in range(8)]
    w_there = lax.ppermute(jnp.stack(w_here), ("zh", "zl"), near)
    attn = lax.all_to_all(merge(parts, rows, 4), "yl", 0, 0, tiled=True)
    places = jnp.stack([core, zl] + [(yl - n) % 4 for n in range(4)]).astype(jnp.int32)
    keep, give = project(places, attn, w_own, w_here, w_there)
    got = turn(give, "c", 2, 1)
    return add_halves(keep, got)


def solution(mesh):
    split = jax.sharding.Mesh(
        mesh.devices.reshape(4, 2, 2, 4, 4, 2), ("zh", "zl", "yh", "x", "yl", "c")
    )
    seq, head = ("zh", "zl", "yh", "x"), ("yl", "c")
    block = P(seq, head)
    return jax.shard_map(
        per_device,
        mesh=split,
        in_specs=(block,) * 6 + (P(head, None),),
        out_specs=(block, block),
        check_vma=False,
    )
```

time: 137 us -> 104 us (0.76)
  waiting for transfers between devices: 45.9 us -> 20.8 us
  blocking collectives: 22.6 us -> 11.4 us
  starting transfers between devices: 51.6 us -> 55 us
  Pallas kernels: 10.6 us -> 12.2 us
    ppermute x12 -> x6, waiting for transfers between devices: 37.9 us -> 9.85 us  [turn(): lax.ppermute(array, axis, [(i, (i + offset) % count) for i in range(count)])]
    all_to_all x1 -> x4, starting transfers between devices: 8.3 us -> 24.5 us  [the longest x1 10.8 us: per_device(): k_first = lax.all_to_all(k_spread, 'zh', 0, 0, tiled=True)]
    ppermute x12 -> x6, starting transfers between devices: 43.3 us -> 27.2 us  [turn(): lax.ppermute(array, axis, [(i, (i + offset) % count) for i in range(count)])]
    all_gather x1, blocking collectives: 22.6 us -> 11.4 us  [per_device(): q_near = lax.all_gather(q_own, 'x', axis=0)]
    ppermute x0 -> x1, starting transfers between devices: none -> 3.29 us  [per_device(): w_there = lax.ppermute(jnp.stack(w_here), ('zh', 'zl'), near)]
    all_to_all x1 -> x4, waiting for transfers between devices: 7.97 us -> 10.9 us  [the longest x1 5.89 us: per_device(): parts = lax.all_to_all(partial, ('x', 'zl'), 0, 0, tiled=True)]
    unnamed x7 -> x0, local copies, waits for them, and re-layouts: 2.55 us -> none
    pallas_call x2 -> x3, Pallas kernels: 7.67 us -> 10 us  [the longest x1 6.73 us: attention(): pl.pallas_call(lambda *refs: attention_body(rows, step_blocks, *refs), ou...]
  transfers between devices with their start and end apart: 13 -> 11, of which waited for: 8 -> 4; matrix products, arithmetic and copies ran while one was open for 2% -> 2% of each run, Pallas kernels for 1% -> 8%
where the time goes in v2:
time: 104 us; the launch traced here: 103 us
  starting transfers between devices  55 us (53%)
  waiting for transfers between devices  20.8 us (20%)
  Pallas kernels  12.2 us (12%)
  blocking collectives  11.4 us (11%)
  local copies, waits for them, and re-layouts  3.2 us (3%)
    ppermute x6, starting transfers between devices, turn(): lax.ppermute(array, axis, [(i, (i + offset) % count) for i in range(count)])  27.2 us
    all_gather x1, blocking collectives, per_device(): q_near = lax.all_gather(q_own, 'x', axis=0)  11.4 us
    all_to_all x1, starting transfers between devices, per_device(): k_first = lax.all_to_all(k_spread, 'zh', 0, 0, tiled=True)  10.8 us
    ppermute x6, waiting for transfers between devices, turn(): lax.ppermute(array, axis, [(i, (i + offset) % count) for i in range(count)])  9.85 us
    pallas_call x1, Pallas kernels, attention(): pl.pallas_call(lambda *refs: attention_body(rows, step_blocks, *refs), ou...  6.73 us
    all_to_all x1, starting transfers between devices, spread(): lax.all_to_all(jnp.broadcast_to(array[None], (count,) + array.shape), axi...  5.9 us
    all_to_all x1, waiting for transfers between devices, per_device(): parts = lax.all_to_all(partial, ('x', 'zl'), 0, 0, tiled=True)  5.89 us
    all_to_all x1, waiting for transfers between devices, per_device(): attn = lax.all_to_all(merge(parts, rows, 4), 'yl', 0, 0, tiled=True)  5.05 us
  transfers between devices with their start and end apart: 11, of which 4 were waited for; matrix products, arithmetic and copies ran while one was open for 2% of the time, Pallas kernels for 8%

profile of v2, /device:TPU:1, one launch (start us, length us, event | category | flops | bytes accessed | tf_op | source)
XLA Modules:
  0.0 103.5 jit_solution(8152370768274691541)
XLA Ops:
  0.6 1.9 %prepare.1 = (bf16[320,128]{1,0:T(8,128)(2,1)}, bf16[640,128]{1,0:T(8,128)(2,1)}, bf16[4,640,128]{2,1,0:T(8,128)(2,1)}) custom-call(bf16[160,128]{1,0:T(8,128)(2,1)} %refs_0_.1, bf16[160,128]{1,0:T(8,128)(2,1)} %refs_1_.1, bf16[160,128]{1,0:T(8,128)(2,1)} %refs_2_.1, bf16[160,128]{1,0:T(8,128)(2,1)} %refs_3_.1, bf16[160,128]{1,0:T(8,128)(2,1)} %refs_4_.1, ...), custom_call_target="tpu_custom_call" | custom-call | tf_op jit(solution)/shard_map/prepare/pallas_call | solution.py:237
  2.5 10.8 %all-to-all-start = ((bf16[4,640,128]{2,1,0:T(8,128)(2,1)}), bf16[4,640,128]{2,1,0:T(8,128)(2,1)S(1)}, u32[]{:S(2)}, u32[]{:S(2)}) async-start(bf16[4,640,128]{2,1,0:T(8,128)(2,1)} %get-tuple-element.15), calls=%async_computation | async-start | bytes 1310720 | tf_op jit(solution)/shard_map/all_to_all | solution.py:267
  13.4 7.4 %collective-permute-start = (bf16[640,128]{1,0:T(8,128)(2,1)}, bf16[640,128]{1,0:T(8,128)(2,1)S(1)}, u32[]{:S(2)}, u32[]{:S(2)}) collective-permute-start(bf16[640,128]{1,0:T(8,128)(2,1)} %get-tuple-element.16), channel_id=1, source_target_pairs={{0,32},{32,0},{1,33},{33,1},{2,34},{34,2},{3,35},{35,3},{4,36},{36... | collective-permute-start | bytes 491528 | tf_op jit(solution)/shard_map/ppermute | solution.py:253
  20.8 11.4 %all-gather = bf16[1280,128]{1,0:T(8,128)(2,1)S(1)} all-gather(bf16[320,128]{1,0:T(8,128)(2,1)} %get-tuple-element.14), channel_id=2, replica_groups=mesh['zh'=4,'zl'=2,'yh'=2,'x'=4,'yl'=4,'c'=2] {'x'}, dimensions={0}, use_global_device_ids=true | all-gather | bytes 409600 | tf_op jit(solution)/shard_map/all_gather | solution.py:269
  32.3 0.0 collective-permute-done
  32.3 0.0 all-to-all-done.refs_3_
  32.3 0.9 broadcast_in_dim.16
  33.2 5.9 %all-to-all-start.1 = ((bf16[4,640,128]{2,1,0:T(8,128)(2,1)}), bf16[4,640,128]{2,1,0:T(8,128)(2,1)S(1)}, u32[]{:S(2)}, u32[]{:S(2)}) async-start(bf16[4,640,128]{2,1,0:T(8,128)(2,1)} %broadcast_in_dim.16), calls=%async_computation.1 | async-start | bytes 1310720 | tf_op jit(solution)/shard_map/all_to_all | solution.py:257
  39.1 3.7 %collective-permute-start.1 = (bf16[4,320,128]{2,1,0:T(8,128)(2,1)S(1)}, bf16[4,320,128]{2,1,0:T(8,128)(2,1)S(1)}, u32[]{:S(2)}, u32[]{:S(2)}) collective-permute-start(bf16[4,320,128]{2,1,0:T(8,128)(2,1)S(1)} %bitcast.13), channel_id=1, source_target_pairs={{0,64},{64,0},{1,65},{65,1},{2,66},{66,2},{3,67},{67,3},{4,68},{68... | collective-permute-start | bytes 983048 | tf_op jit(solution)/shard_map/ppermute | solution.py:253
  42.8 1.2 %fusion.2 = (bf16[64,1536]{1,0:T(8,128)(2,1)S(1)}, bf16[64,1536]{1,0:T(8,128)(2,1)S(1)}, bf16[64,1536]{1,0:T(8,128)(2,1)S(1)}) fusion(bf16[128,6144]{1,0:T(8,128)(2,1)} %param.13, s32[]{:T(128)S(6)} %select_n.66, s32[]{:T(128)S(6)} %select_n.72, s32[]{:T(128)S(6)} %select_n.70, s32[]{:T(128)S(6)} %select_n.68), kind=kLoop, calls=%fused_computation.6 | loop fusion | bytes 1179664 | tf_op jit(solution)/shard_map/dynamic_slice | solution.py:276
  44.0 2.3 %collective-permute-start.2 = (bf16[64,1536]{1,0:T(8,128)(2,1)S(1)}, bf16[64,1536]{1,0:T(8,128)(2,1)S(1)}, u32[]{:S(2)}, u32[]{:S(2)}) collective-permute-start(bf16[64,1536]{1,0:T(8,128)(2,1)S(1)} %get-tuple-element.28), channel_id=1, source_target_pairs={{0,2},{2,4},{4,6},{6,0},{1,3},{3,5},{5,7},{7,1},{8,10},{10,12},{12... | collective-permute-start | bytes 589832 | tf_op jit(solution)/shard_map/ppermute | solution.py:253
  46.3 2.4 %collective-permute-start.3 = (bf16[64,1536]{1,0:T(8,128)(2,1)S(1)}, bf16[64,1536]{1,0:T(8,128)(2,1)S(1)}, u32[]{:S(2)}, u32[]{:S(2)}) collective-permute-start(bf16[64,1536]{1,0:T(8,128)(2,1)S(1)} %get-tuple-element.27), channel_id=1, source_target_pairs={{0,4},{2,6},{4,0},{6,2},{1,5},{3,7},{5,1},{7,3},{8,12},{10,14},{12... | collective-permute-start | bytes 589832 | tf_op jit(solution)/shard_map/ppermute | solution.py:253
  48.8 4.3 %collective-permute-start.4 = (bf16[64,1536]{1,0:T(8,128)(2,1)S(1)}, bf16[64,1536]{1,0:T(8,128)(2,1)S(1)}, u32[]{:S(2)}, u32[]{:S(2)}) collective-permute-start(bf16[64,1536]{1,0:T(8,128)(2,1)S(1)} %get-tuple-element.26), channel_id=1, source_target_pairs={{0,6},{2,0},{4,2},{6,4},{1,7},{3,1},{5,3},{7,5},{8,14},{10,8},{12,... | collective-permute-start | bytes 589832 | tf_op jit(solution)/shard_map/ppermute | solution.py:253
  53.1 8.4 %collective-permute-done.1.refs_2_ = bf16[4,320,128]{2,1,0:T(8,128)(2,1)S(1)} collective-permute-done((bf16[4,320,128]{2,1,0:T(8,128)(2,1)S(1)}, bf16[4,320,128]{2,1,0:T(8,128)(2,1)S(1)}, u32[]{:S(2)}, u32[]{:S(2)}) %collective-permute-start.1) | collective-permute-done | bytes 327712 | tf_op jit(solution)/shard_map/ppermute | solution.py:253
  61.4 0.0 all-to-all-done.1.refs_4_
  61.4 6.7 %attention.1 = bf16[8,336,128]{2,1,0:T(8,128)(2,1)} custom-call(s32[8]{0:T(128)S(1)} %fusion.1.refs_0_, bf16[4,320,128]{2,1,0:T(8,128)(2,1)S(1)} %bitcast.14, bf16[4,320,128]{2,1,0:T(8,128)(2,1)S(1)} %collective-permute-done.1.refs_2_, bf16[4,640,128]{2,1,0:T(8,128)(2,1)S(1)} %all-to-all-done.refs_3_, bf16[4,640,128]{2,1,0:T(8,128)(2,1)S(1)} %all-to-all-done.1.refs_4_), custom_call_target="tpu_custom_call" | custom-call | flops 2516582400 | bytes 4000000 | tf_op jit(solution)/shard_map/attention/pallas_call | solution.py:117
  68.2 0.0 collective-permute-done.2.refs_3_
  68.2 0.0 collective-permute-done.3.refs_4_
  68.2 0.0 collective-permute-done.4.refs_5_
  68.2 3.6 %all-to-all-start.2 = ((bf16[8,336,128]{2,1,0:T(8,128)(2,1)}), bf16[8,336,128]{2,1,0:T(8,128)(2,1)S(1)}, u32[]{:S(2)}, u32[]{:S(2)}) async-start(bf16[8,336,128]{2,1,0:T(8,128)(2,1)} %attention.1), calls=%async_computation.2 | async-start | bytes 1376256 | tf_op jit(solution)/shard_map/all_to_all | solution.py:285
  71.7 0.1 pad_maximum_fusion
  71.8 3.3 %collective-permute-start.5 = (bf16[3,64,1536]{2,1,0:T(8,128)(2,1)S(1)}, bf16[3,64,1536]{2,1,0:T(8,128)(2,1)S(1)}, u32[]{:S(2)}, u32[]{:S(2)}) collective-permute-start(bf16[3,64,1536]{2,1,0:T(8,128)(2,1)S(1)} %pad_maximum_fusion), channel_id=1, source_target_pairs={{0,448},{64,128},{128,64},{192,256},{256,192},{320,384},{384,320},... | collective-permute-start | bytes 1769480 | tf_op jit(solution)/shard_map/ppermute | solution.py:287
  75.1 5.9 %all-to-all-done.2.refs_0_ = bf16[8,336,128]{2,1,0:T(8,128)(2,1)S(1)} async-done(((bf16[8,336,128]{2,1,0:T(8,128)(2,1)}), bf16[8,336,128]{2,1,0:T(8,128)(2,1)S(1)}, u32[]{:S(2)}, u32[]{:S(2)}) %all-to-all-start.2) | async-done | bytes 688160 | tf_op jit(solution)/shard_map/all_to_all | solution.py:285
  81.0 1.4 %merge.1 = bf16[4,320,128]{2,1,0:T(8,128)(2,1)} custom-call(bf16[8,336,128]{2,1,0:T(8,128)(2,1)S(1)} %all-to-all-done.2.refs_0_), custom_call_target="tpu_custom_call" | custom-call | tf_op jit(solution)/shard_map/merge/pallas_call | solution.py:160
  82.4 4.2 %all-to-all-start.3 = ((bf16[4,320,128]{2,1,0:T(8,128)(2,1)}), bf16[4,320,128]{2,1,0:T(8,128)(2,1)S(1)}, u32[]{:S(2)}, u32[]{:S(2)}) async-start(bf16[4,320,128]{2,1,0:T(8,128)(2,1)} %merge.1), calls=%async_computation.3 | async-start | bytes 655360 | tf_op jit(solution)/shard_map/all_to_all | solution.py:288
  86.7 0.1 stack.39.refs_0_
  86.7 1.0 constant_dynamic-slice_fusion.refs_2_
  87.8 0.0 collective-permute-done.5.refs_6_
  87.8 5.0 %all-to-all-done.3.refs_1_ = bf16[4,320,128]{2,1,0:T(8,128)(2,1)S(1)} async-done(((bf16[4,320,128]{2,1,0:T(8,128)(2,1)}), bf16[4,320,128]{2,1,0:T(8,128)(2,1)S(1)}, u32[]{:S(2)}, u32[]{:S(2)}) %all-to-all-start.3) | async-done | bytes 327712 | tf_op jit(solution)/shard_map/all_to_all | solution.py:288
  92.8 1.3 %project.1 = (f32[320,768]{1,0:T(8,128)S(1)}, bf16[320,768]{1,0:T(8,128)(2,1)S(1)}) custom-call(s32[6]{0:T(128)S(1)} %stack.39.refs_0_, bf16[4,320,128]{2,1,0:T(8,128)(2,1)S(1)} %all-to-all-done.3.refs_1_, bf16[128,1536]{1,0:T(8,128)(2,1)S(1)} %constant_dynamic-slice_fusion.refs_2_, bf16[64,1536]{1,0:T(8,128)(2,1)S(1)} %collective-permute-done.2.refs_3_, ...), custom_call_target="tpu_custom_call" | custom-call | flops 503316480 | bytes 4000000 | tf_op jit(solution)/shard_map/project/pallas_call | solution.py:188
  94.2 7.0 %collective-permute-start.6 = (bf16[320,768]{1,0:T(8,128)(2,1)S(1)}, bf16[320,768]{1,0:T(8,128)(2,1)S(1)}, u32[]{:S(2)}, u32[]{:S(2)}) collective-permute-start(bf16[320,768]{1,0:T(8,128)(2,1)S(1)} %get-tuple-element.25), channel_id=1, source_target_pairs={{0,1},{1,0},{2,3},{3,2},{4,5},{5,4},{6,7},{7,6},{8,9},{9,8},{10,11... | collective-permute-start | bytes 1474568 | tf_op jit(solution)/shard_map/ppermute | solution.py:253
  101.2 1.5 %collective-permute-done.6.refs_1_ = bf16[320,768]{1,0:T(8,128)(2,1)S(1)} collective-permute-done((bf16[320,768]{1,0:T(8,128)(2,1)S(1)}, bf16[320,768]{1,0:T(8,128)(2,1)S(1)}, u32[]{:S(2)}, u32[]{:S(2)}) %collective-permute-start.6) | collective-permute-done | bytes 491552 | tf_op jit(solution)/shard_map/ppermute | solution.py:253
  102.6 0.8 add_halves.1
  (1 shorter events, 0.0 us)
Async XLA Ops:
  2.5 29.8 %all-to-all-start = ((bf16[4,640,128]{2,1,0:T(8,128)(2,1)}), bf16[4,640,128]{2,1,0:T(8,128)(2,1)S(1)}, u32[]{:S(2)}, u32[]{:S(2)}) async-start(bf16[4,640,128]{2,1,0:T(8,128)(2,1)} %get-tuple-element.15), calls=%async_computation | async-start | bytes 1310720 | tf_op jit(solution)/shard_map/all_to_all | solution.py:267
  13.4 18.9 %collective-permute-start = (bf16[640,128]{1,0:T(8,128)(2,1)}, bf16[640,128]{1,0:T(8,128)(2,1)S(1)}, u32[]{:S(2)}, u32[]{:S(2)}) collective-permute-start(bf16[640,128]{1,0:T(8,128)(2,1)} %get-tuple-element.16), channel_id=1, source_target_pairs={{0,32},{32,0},{1,33},{33,1},{2,34},{34,2},{3,35},{35,3},{4,36},{36... | collective-permute-start | bytes 491528 | tf_op jit(solution)/shard_map/ppermute | solution.py:253
  33.2 28.2 %all-to-all-start.1 = ((bf16[4,640,128]{2,1,0:T(8,128)(2,1)}), bf16[4,640,128]{2,1,0:T(8,128)(2,1)S(1)}, u32[]{:S(2)}, u32[]{:S(2)}) async-start(bf16[4,640,128]{2,1,0:T(8,128)(2,1)} %broadcast_in_dim.16), calls=%async_computation.1 | async-start | bytes 1310720 | tf_op jit(solution)/shard_map/all_to_all | solution.py:257
  39.1 22.3 %collective-permute-start.1 = (bf16[4,320,128]{2,1,0:T(8,128)(2,1)S(1)}, bf16[4,320,128]{2,1,0:T(8,128)(2,1)S(1)}, u32[]{:S(2)}, u32[]{:S(2)}) collective-permute-start(bf16[4,320,128]{2,1,0:T(8,128)(2,1)S(1)} %bitcast.13), channel_id=1, source_target_pairs={{0,64},{64,0},{1,65},{65,1},{2,66},{66,2},{3,67},{67,3},{4,68},{68... | collective-permute-start | bytes 983048 | tf_op jit(solution)/shard_map/ppermute | solution.py:253
  44.0 24.1 %collective-permute-start.2 = (bf16[64,1536]{1,0:T(8,128)(2,1)S(1)}, bf16[64,1536]{1,0:T(8,128)(2,1)S(1)}, u32[]{:S(2)}, u32[]{:S(2)}) collective-permute-start(bf16[64,1536]{1,0:T(8,128)(2,1)S(1)} %get-tuple-element.28), channel_id=1, source_target_pairs={{0,2},{2,4},{4,6},{6,0},{1,3},{3,5},{5,7},{7,1},{8,10},{10,12},{12... | collective-permute-start | bytes 589832 | tf_op jit(solution)/shard_map/ppermute | solution.py:253
  46.3 21.8 %collective-permute-start.3 = (bf16[64,1536]{1,0:T(8,128)(2,1)S(1)}, bf16[64,1536]{1,0:T(8,128)(2,1)S(1)}, u32[]{:S(2)}, u32[]{:S(2)}) collective-permute-start(bf16[64,1536]{1,0:T(8,128)(2,1)S(1)} %get-tuple-element.27), channel_id=1, source_target_pairs={{0,4},{2,6},{4,0},{6,2},{1,5},{3,7},{5,1},{7,3},{8,12},{10,14},{12... | collective-permute-start | bytes 589832 | tf_op jit(solution)/shard_map/ppermute | solution.py:253
  48.8 19.4 %collective-permute-start.4 = (bf16[64,1536]{1,0:T(8,128)(2,1)S(1)}, bf16[64,1536]{1,0:T(8,128)(2,1)S(1)}, u32[]{:S(2)}, u32[]{:S(2)}) collective-permute-start(bf16[64,1536]{1,0:T(8,128)(2,1)S(1)} %get-tuple-element.26), channel_id=1, source_target_pairs={{0,6},{2,0},{4,2},{6,4},{1,7},{3,1},{5,3},{7,5},{8,14},{10,8},{12,... | collective-permute-start | bytes 589832 | tf_op jit(solution)/shard_map/ppermute | solution.py:253
  68.2 12.8 %all-to-all-start.2 = ((bf16[8,336,128]{2,1,0:T(8,128)(2,1)}), bf16[8,336,128]{2,1,0:T(8,128)(2,1)S(1)}, u32[]{:S(2)}, u32[]{:S(2)}) async-start(bf16[8,336,128]{2,1,0:T(8,128)(2,1)} %attention.1), calls=%async_computation.2 | async-start | bytes 1376256 | tf_op jit(solution)/shard_map/all_to_all | solution.py:285
  71.8 16.0 %collective-permute-start.5 = (bf16[3,64,1536]{2,1,0:T(8,128)(2,1)S(1)}, bf16[3,64,1536]{2,1,0:T(8,128)(2,1)S(1)}, u32[]{:S(2)}, u32[]{:S(2)}) collective-permute-start(bf16[3,64,1536]{2,1,0:T(8,128)(2,1)S(1)} %pad_maximum_fusion), channel_id=1, source_target_pairs={{0,448},{64,128},{128,64},{192,256},{256,192},{320,384},{384,320},... | collective-permute-start | bytes 1769480 | tf_op jit(solution)/shard_map/ppermute | solution.py:287
  82.4 10.4 %all-to-all-start.3 = ((bf16[4,320,128]{2,1,0:T(8,128)(2,1)}), bf16[4,320,128]{2,1,0:T(8,128)(2,1)S(1)}, u32[]{:S(2)}, u32[]{:S(2)}) async-start(bf16[4,320,128]{2,1,0:T(8,128)(2,1)} %merge.1), calls=%async_computation.3 | async-start | bytes 655360 | tf_op jit(solution)/shard_map/all_to_all | solution.py:288
  94.2 8.5 %collective-permute-start.6 = (bf16[320,768]{1,0:T(8,128)(2,1)S(1)}, bf16[320,768]{1,0:T(8,128)(2,1)S(1)}, u32[]{:S(2)}, u32[]{:S(2)}) collective-permute-start(bf16[320,768]{1,0:T(8,128)(2,1)S(1)} %get-tuple-element.25), channel_id=1, source_target_pairs={{0,1},{1,0},{2,3},{3,2},{4,5},{5,4},{6,7},{7,6},{8,9},{9,8},{10,11... | collective-permute-start | bytes 1474568 | tf_op jit(solution)/shard_map/ppermute | solution.py:253

commit v3 on v2

v3 whole, which is shorter than its diff:
```python
import jax, jax.numpy as jnp
from jax import lax
from jax.sharding import PartitionSpec as P
from jax.experimental import pallas as pl
from jax.experimental.pallas import tpu as pltpu

HD = 128
SCALE = HD ** -0.5
LOG2E = 1.4426950408889634
STAT = 16
F32 = jnp.float32
BF16 = jnp.bfloat16


def dot_nt(a, b):
    return lax.dot_general(a, b, (((1,), (1,)), ((), ())), preferred_element_type=F32)


def dot_nn(a, b):
    return jnp.dot(a, b, preferred_element_type=F32)


def three_parts(value):
    high = value.astype(BF16).astype(F32)
    rest = value - high
    mid = rest.astype(BF16).astype(F32)
    return high, mid, (rest - mid)


WHOLE = pl.BlockSpec(memory_space=pltpu.VMEM)
SCALAR = pl.BlockSpec(memory_space=pltpu.SMEM)


def limit(mib):
    return pltpu.CompilerParams(vmem_limit_bytes=mib * 1024 * 1024)


def stat_rows(stats, rows):
    lane = lax.broadcasted_iota(jnp.int32, (rows, HD), 1)
    pick_row = lax.broadcasted_iota(jnp.int32, (STAT, HD), 0)
    pick_lane = lax.broadcasted_iota(jnp.int32, (STAT, HD), 1)
    half = STAT // 2
    low = jnp.where((pick_row == pick_lane) & (pick_row < half), 1.0, 0.0).astype(BF16)
    high = jnp.where((pick_row == pick_lane + half) & (pick_lane < half), 1.0, 0.0).astype(BF16)
    table = jnp.zeros((rows, HD), F32)
    for n, stat in enumerate(stats):
        table = jnp.where(lane == n, stat, table)
    table = jnp.concatenate([table, jnp.zeros((2 * HD - rows, HD), F32)]).astype(BF16)
    return (dot_nt(low, table[:HD]) + dot_nt(high, table[HD:])).astype(BF16)


def stat_columns(block, rows, first):
    pick_row = lax.broadcasted_iota(jnp.int32, (STAT, HD), 0)

    def turned(at):
        pick = jnp.where((pick_row >= at) & (pick_row < at + 3), 1.0, 0.0).astype(BF16)
        return lax.dot_general(block, pick, (((0,), (0,)), ((), ())), preferred_element_type=F32)

    return jnp.concatenate([turned(first), turned(first + STAT // 2)[: rows - HD]])


def attention_tile(q_ref, kk, vv, span):
    scores = dot_nt(q_ref[span, HD:], kk[:, :HD])
    slope = dot_nt(q_ref[span, :], kk[...])
    top = jnp.max(scores, axis=1, keepdims=True)
    weights = jnp.exp2((scores - top) * (SCALE * LOG2E))
    total = jnp.sum(weights, axis=1, keepdims=True)
    sloped = weights * slope
    grad = jnp.sum(sloped, axis=1, keepdims=True)
    both = dot_nn(weights.astype(BF16), vv[...])
    extra = dot_nn(sloped.astype(BF16), vv[:, :HD])
    inverse = 1.0 / total
    mean = both[:, :HD] * inverse
    slope_mean = grad * (SCALE * inverse)
    tangent = (extra * SCALE + both[:, HD:]) * inverse - slope_mean * mean
    return mean, tangent, top * SCALE + jnp.log(total), slope_mean


def attention_body(rows, step_blocks, q_ref, ka_ref, kb_ref, out_ref, qq, kk, vv):
    blocks = q_ref.shape[0]
    for b in range(blocks):
        span = pl.ds(b * rows, rows)
        qq[span, :HD] = q_ref[b, rows:]
        qq[span, HD:] = q_ref[b, :rows]
    for n, k_ref in enumerate((ka_ref, kb_ref)):
        for b in range(k_ref.shape[0]):
            span = pl.ds((n * k_ref.shape[0] + b) * rows, rows)
            kk[span, :HD] = k_ref[b, :rows]
            vv[span, :HD] = k_ref[b, rows:2 * rows]
            kk[span, HD:] = k_ref[b, 2 * rows:3 * rows]
            vv[span, HD:] = k_ref[b, 3 * rows:]
    span_rows = step_blocks * rows

    def step(i, carry):
        span = pl.ds(pl.multiple_of(i * span_rows, span_rows), span_rows)
        mean, tangent, log, slope = attention_tile(qq, kk, vv, span)
        stats = three_parts(log) + three_parts(slope)
        for b in range(step_blocks):
            part = slice(b * rows, (b + 1) * rows)
            at = i * step_blocks + b
            out_ref[at, :rows, :] = mean[part].astype(BF16)
            out_ref[at, rows:2 * rows, :] = tangent[part].astype(BF16)
            out_ref[at, 2 * rows:, :] = stat_rows([s[part] for s in stats], rows)
        return carry

    lax.fori_loop(0, blocks // step_blocks, step, 0)


def attention(queries, keys, rows, step_blocks=4):
    blocks, nkeys = queries.shape[0], sum(p.shape[0] for p in keys) * rows
    work = blocks * rows * nkeys * HD
    return pl.pallas_call(
        lambda *refs: attention_body(rows, step_blocks, *refs),
        out_shape=jax.ShapeDtypeStruct((blocks, 2 * rows + STAT, HD), BF16),
        in_specs=[WHOLE] * 3,
        out_specs=WHOLE,
        scratch_shapes=[
            pltpu.VMEM((blocks * rows, 2 * HD), BF16),
            pltpu.VMEM((nkeys, 2 * HD), BF16),
            pltpu.VMEM((nkeys, 2 * HD), BF16),
        ],
        compiler_params=limit(32),
        cost_estimate=pl.CostEstimate(flops=12 * work, bytes_accessed=4000000, transcendentals=work // HD),
        name="attention",
    )(queries, *keys)


def merged(blocks, rows):
    logs = [stat_columns(block[2 * rows:, :], rows, 0) for block in blocks]
    slopes = [stat_columns(block[2 * rows:, :], rows, 3) for block in blocks]
    top = logs[0]
    for log in logs[1:]:
        top = jnp.maximum(top, log)
    shares = [jnp.exp(log - top) for log in logs]
    total = sum(shares[1:], shares[0])
    inverse = 1.0 / total
    slope_mean = sum([s * g for s, g in zip(shares[1:], slopes[1:])], shares[0] * slopes[0]) * inverse
    mean = jnp.zeros((rows, HD), F32)
    tangent = jnp.zeros((rows, HD), F32)
    for block, share, slope in zip(blocks, shares, slopes):
        one = block[:rows, :].astype(F32)
        mean += share * one
        tangent += share * (block[rows:2 * rows, :].astype(F32) + (slope - slope_mean) * one)
    return mean * inverse, tangent * inverse, top + jnp.log(total), slope_mean


def merge_body(rows, part_ref, out_ref):
    mean, tangent, _, _ = merged([part_ref[b] for b in range(part_ref.shape[0])], rows)
    out_ref[:rows, :] = mean.astype(BF16)
    out_ref[rows:, :] = tangent.astype(BF16)


def merge(parts, rows):
    return pl.pallas_call(
        lambda *refs: merge_body(rows, *refs),
        out_shape=jax.ShapeDtypeStruct((2 * rows, HD), BF16),
        in_specs=[WHOLE],
        out_specs=WHOLE,
        compiler_params=limit(12),
        name="merge",
    )(parts)


def cut_body(columns, at_ref, own_ref, next_ref, half_ref, keep_ref, give_ref):
    core = at_ref[0]
    mine = pl.ds(pl.multiple_of(core * columns, HD), columns)
    other = pl.ds(pl.multiple_of((1 - core) * columns, HD), columns)
    for out_ref, span in ((keep_ref, mine), (give_ref, other)):
        at = 0
        for ref in (own_ref, next_ref, half_ref):
            out_ref[at:at + ref.shape[0], :] = ref[:, span]
            at += ref.shape[0]


def cut_columns(places, weights):
    columns = weights[0].shape[1] // 2
    one = jax.ShapeDtypeStruct((sum(w.shape[0] for w in weights), columns), BF16)
    return pl.pallas_call(
        lambda *refs: cut_body(columns, *refs),
        out_shape=(one, one),
        in_specs=[SCALAR] + [WHOLE] * len(weights),
        out_specs=(WHOLE, WHOLE),
        compiler_params=limit(8),
        cost_estimate=pl.CostEstimate(flops=1000000, bytes_accessed=4000000, transcendentals=0),
        name="cut_columns",
    )(places, *weights)


def project_body(rows, at_ref, attn_ref, keep_ref, got_ref, others_ref, out_ref, tan_ref, left, right):
    core, half, part = at_ref[0], at_ref[1], HD // 2
    for c, ref in enumerate((keep_ref, got_ref)):
        first, theirs = 4 * c, (HD + part) * c
        for n in range(4):
            head = 2 * at_ref[2 + n] + (core if c == 0 else 1 - core)
            left[:, (first + n) * HD:(first + n + 1) * HD] = attn_ref[head]
        base = first * HD
        right[base:base + 2 * HD, :] = ref[:2 * HD, :]
        right[base + 2 * HD:base + 3 * HD, :] = others_ref[theirs:theirs + HD, :]
        low = base + 3 * HD
        right[pl.ds(pl.multiple_of(low + half * part, part), part), :] = ref[2 * HD:, :]
        right[pl.ds(pl.multiple_of(low + (1 - half) * part, part), part), :] = others_ref[theirs + HD:theirs + HD + part, :]
    total = dot_nn(left[...], right[...])
    out_ref[...] = total[:rows].astype(BF16)
    tan_ref[...] = total[rows:].astype(BF16)


def project(places, attn, keep, got, others):
    heads, both, _ = attn.shape
    columns = keep.shape[1]
    one = jax.ShapeDtypeStruct((both // 2, columns), BF16)
    return pl.pallas_call(
        lambda *refs: project_body(both // 2, *refs),
        out_shape=(one, one),
        in_specs=[SCALAR] + [WHOLE] * 4,
        out_specs=(WHOLE, WHOLE),
        scratch_shapes=[
            pltpu.VMEM((both, heads * HD), BF16),
            pltpu.VMEM((heads * HD, columns), BF16),
        ],
        compiler_params=limit(12),
        cost_estimate=pl.CostEstimate(flops=2 * both * heads * HD * columns, bytes_accessed=4000000, transcendentals=0),
        name="project",
    )(places, attn, keep, got, others)


def prepare_body(rows, copies, q_ref, k_ref, v_ref, qt_ref, kt_ref, vt_ref, spread_ref, keys_ref):
    for n, ref in enumerate((q_ref, qt_ref)):
        value = ref[...]
        for m in range(copies):
            spread_ref[m, pl.ds(n * rows, rows), :] = value
    for n, ref in enumerate((k_ref, v_ref, kt_ref, vt_ref)):
        keys_ref[pl.ds(n * rows, rows), :] = ref[...]


def prepare(arrays, copies):
    rows = arrays[0].shape[0]
    return pl.pallas_call(
        lambda *refs: prepare_body(rows, copies, *refs),
        out_shape=(
            jax.ShapeDtypeStruct((copies, 2 * rows, HD), BF16),
            jax.ShapeDtypeStruct((4 * rows, HD), BF16),
        ),
        grid=(1,),
        in_specs=[pl.BlockSpec((rows, HD), lambda i: (0, 0))] * 6,
        out_specs=(WHOLE,) * 2,
        compiler_params=limit(56),
        name="prepare",
    )(*arrays)


def turn(array, axis, count, offset):
    return lax.ppermute(array, axis, [(i, (i + offset) % count) for i in range(count)])


def per_device(queries, key_vectors, value_vectors, query_tangent, key_tangent, value_tangent, out_weight):
    rows = queries.shape[0]
    zl, yl, core = (lax.axis_index(name) for name in ("zl", "yl", "c"))
    columns = out_weight.shape[1] // 4

    arrays = (queries, key_vectors, value_vectors, query_tangent, key_tangent, value_tangent)
    q_spread, k_own = prepare(arrays, 8)
    k_far = turn(k_own, "yh", 2, 1)
    q_all = lax.all_to_all(q_spread, ("x", "zl"), 0, 0, tiled=True)
    k_first = lax.all_gather(k_own, "zh", axis=0)
    k_first, q_all, k_far = lax.optimization_barrier((k_first, q_all, k_far))
    k_second = jnp.broadcast_to(k_far[None], (4,) + k_far.shape)
    k_second = lax.all_to_all(k_second, "zh", 0, 0, tiled=True)

    def weight_of(n, first, height):
        at = (first, ((yl + n) % 4) * columns)
        return lax.dynamic_slice(out_weight, at, (height, columns))

    step = jnp.where(zl == 0, 1, 3)
    ring = [(4 * z + y, 4 * z + (y + (1, 3)[z]) % 4) for z in range(2) for y in range(4)]
    w_own = weight_of(0, 0, HD)
    w_next = lax.ppermute(weight_of(step, 0, HD), ("zl", "yl"), ring)
    w_half = turn(weight_of(2, zl * (HD // 2), HD // 2), "yl", 4, 2)

    partial = attention(q_all, (k_first, k_second), rows)
    partial, w_next, w_half = lax.optimization_barrier((partial, w_next, w_half))
    parts = lax.all_to_all(partial, ("x", "zl"), 0, 0, tiled=True)
    heads = [yl, yl - step, yl + step, yl + 2]
    places = jnp.stack([core, zl] + [head % 4 for head in heads]).astype(jnp.int32)
    keep, give = cut_columns(places, (w_own, w_next, w_half))
    got = turn(give, "c", 2, 1)
    near = [(z, (z + 1) % 8 if z % 2 else (z - 1) % 8) for z in range(8)]
    others = lax.ppermute(jnp.concatenate([keep[HD:], got[HD:]]), ("zh", "zl"), near)
    attn = lax.all_gather(merge(parts, rows), ("yl", "c"), axis=0)
    return project(places, attn, keep, got, others)


def solution(mesh):
    split = jax.sharding.Mesh(
        mesh.devices.reshape(4, 2, 2, 4, 4, 2), ("zh", "zl", "yh", "x", "yl", "c")
    )
    seq, head = ("zh", "zl", "yh", "x"), ("yl", "c")
    block = P(seq, head)
    return jax.shard_map(
        per_device,
        mesh=split,
        in_specs=(block,) * 6 + (P(head, None),),
        out_specs=(block, block),
        check_vma=False,
    )
```

time: 104 us -> 103 us (level)
  blocking collectives: 11.4 us -> 36.5 us
  starting transfers between devices: 55 us -> 37.7 us
  waiting for transfers between devices: 20.8 us -> 13.1 us
    all_gather x1 -> x2, blocking collectives: 11.4 us -> 36.5 us  [the longest x1 19.5 us: per_device(): k_first = lax.all_gather(k_own, 'zh', axis=0)]
    ppermute x6 -> x3, starting transfers between devices: 27.2 us -> 12.1 us  [turn(): lax.ppermute(array, axis, [(i, (i + offset) % count) for i in range(count)])]
    all_to_all x3 -> x2, starting transfers between devices: 21 us -> 12.7 us  [the longest x1 6.79 us: per_device(): q_all = lax.all_to_all(q_spread, ('x', 'zl'), 0, 0, tiled=True)]
    ppermute x6 -> x3, waiting for transfers between devices: 9.85 us -> 2.23 us  [turn(): lax.ppermute(array, axis, [(i, (i + offset) % count) for i in range(count)])]
    all_to_all x1, waiting for transfers between devices: 5.89 us -> 0.01 us  [per_device(): parts = lax.all_to_all(partial, ('x', 'zl'), 0, 0, tiled=True)]
    all_to_all x3 -> x2, waiting for transfers between devices: 5.05 us -> 10.9 us  [the longest x1 10.9 us: per_device(): k_second = lax.all_to_all(k_second, 'zh', 0, 0, tiled=True)]
    ppermute x1 -> x2, starting transfers between devices: 3.29 us -> 8.51 us  [the longest x1 6.04 us: per_device(): lax.ppermute(jnp.concatenate([keep[HD:], got[HD:]]), ('zh', 'zl'), near)]
  transfers between devices with their start and end apart: 11 -> 8, of which waited for: 4 -> 3; matrix products, arithmetic and copies ran while one was open for 2% -> 2% of each run, Pallas kernels for 8% -> 7%
where the time goes in v3:
time: 103 us
  starting transfers between devices  37.7 us (37%)
  blocking collectives  36.5 us (35%)
  waiting for transfers between devices  13.1 us (13%)
  Pallas kernels  11.4 us (11%)
  local copies, waits for them, and re-layouts  3.17 us (3%)
    all_gather x1, blocking collectives, per_device(): k_first = lax.all_gather(k_own, 'zh', axis=0)  19.5 us
    all_gather x1, blocking collectives, per_device(): attn = lax.all_gather(merge(parts, rows), ('yl', 'c'), axis=0)  17 us
    ppermute x3, starting transfers between devices, turn(): lax.ppermute(array, axis, [(i, (i + offset) % count) for i in range(count)])  12.1 us
    all_to_all x1, waiting for transfers between devices, per_device(): k_second = lax.all_to_all(k_second, 'zh', 0, 0, tiled=True)  10.9 us
    all_to_all x1, starting transfers between devices, per_device(): q_all = lax.all_to_all(q_spread, ('x', 'zl'), 0, 0, tiled=True)  6.79 us
    pallas_call x1, Pallas kernels, attention(): pl.pallas_call(lambda *refs: attention_body(rows, step_blocks, *refs), ou...  6.13 us
    ppermute x1, starting transfers between devices, per_device(): lax.ppermute(jnp.concatenate([keep[HD:], got[HD:]]), ('zh', 'zl'), near)  6.04 us
    all_to_all x1, starting transfers between devices, per_device(): k_second = lax.all_to_all(k_second, 'zh', 0, 0, tiled=True)  5.93 us
  transfers between devices with their start and end apart: 8, of which 3 were waited for; matrix products, arithmetic and copies ran while one was open for 2% of the time, Pallas kernels for 7%

profile of v3, /device:TPU:1, one launch (start us, length us, event | category | flops | bytes accessed | tf_op | source)
XLA Modules:
  0.0 102.5 jit_solution(8783975738627071126)
XLA Ops:
  0.6 1.8 %prepare.1 = (bf16[8,320,128]{2,1,0:T(8,128)(2,1)}, bf16[640,128]{1,0:T(8,128)(2,1)}) custom-call(bf16[160,128]{1,0:T(8,128)(2,1)} %refs_0_.1, bf16[160,128]{1,0:T(8,128)(2,1)} %refs_1_.1, bf16[160,128]{1,0:T(8,128)(2,1)} %refs_2_.1, bf16[160,128]{1,0:T(8,128)(2,1)} %refs_3_.1, bf16[160,128]{1,0:T(8,128)(2,1)} %refs_4_.1, bf16[160,128]{1,0:T(8,128)(2,1)} %refs_5_.1), custom_call_target="tpu_custom_call" | custom-call | tf_op jit(solution)/shard_map/prepare/pallas_call | solution.py:237
  2.5 0.0 copy-start
  2.5 6.8 %all-to-all-start = ((bf16[8,320,128]{2,1,0:T(8,128)(2,1)}), bf16[8,320,128]{2,1,0:T(8,128)(2,1)S(1)}, u32[]{:S(2)}, u32[]{:S(2)}) async-start(bf16[8,320,128]{2,1,0:T(8,128)(2,1)} %get-tuple-element.13), calls=%async_computation | async-start | bytes 1310720 | tf_op jit(solution)/shard_map/all_to_all | solution.py:263
  9.3 0.0 copy-done
  9.3 7.5 %collective-permute-start = (bf16[640,128]{1,0:T(8,128)(2,1)S(1)}, bf16[640,128]{1,0:T(8,128)(2,1)S(1)}, u32[]{:S(2)}, u32[]{:S(2)}) collective-permute-start(bf16[640,128]{1,0:T(8,128)(2,1)S(1)} %copy-done), channel_id=1, source_target_pairs={{0,32},{32,0},{1,33},{33,1},{2,34},{34,2},{3,35},{35,3},{4,36},{36... | collective-permute-start | bytes 491528 | tf_op jit(solution)/shard_map/ppermute | solution.py:252
  16.7 19.5 %all-gather = bf16[2560,128]{1,0:T(8,128)(2,1)S(1)} all-gather(bf16[640,128]{1,0:T(8,128)(2,1)S(1)} %copy-done), channel_id=2, replica_groups=mesh['zh'=4,'zl'=2,'yh'=2,'x'=4,'yl'=4,'c'=2] {'zh'}, dimensions={0}, use_global_device_ids=true | all-gather | bytes 819200 | tf_op jit(solution)/shard_map/all_gather | solution.py:264
  36.2 0.0 collective-permute-done
  36.2 0.0 all-to-all-done.refs_0_
  36.2 0.9 broadcast_in_dim.2
  37.2 5.9 %all-to-all-start.1 = ((bf16[4,640,128]{2,1,0:T(8,128)(2,1)}), bf16[4,640,128]{2,1,0:T(8,128)(2,1)S(1)}, u32[]{:S(2)}, u32[]{:S(2)}) async-start(bf16[4,640,128]{2,1,0:T(8,128)(2,1)} %broadcast_in_dim.2), calls=%async_computation.1 | async-start | bytes 1310720 | tf_op jit(solution)/shard_map/all_to_all | solution.py:267
  43.1 1.2 %constant_dynamic-slice_fusion = (bf16[128,1536]{1,0:T(8,128)(2,1)S(1)}, bf16[128,1536]{1,0:T(8,128)(2,1)S(1)}) fusion(bf16[128,6144]{1,0:T(8,128)(2,1)} %param.13, s32[]{:T(128)S(6)} %select_n.49, s32[]{:T(128)S(6)} %select_n.46), kind=kLoop, calls=%fused_computation.1 | loop fusion | bytes 1572872 | tf_op jit(solution)/shard_map/dynamic_slice | solution.py:271
  44.3 2.5 %collective-permute-start.1 = (bf16[128,1536]{1,0:T(8,128)(2,1)S(1)}, bf16[128,1536]{1,0:T(8,128)(2,1)S(1)}, u32[]{:S(2)}, u32[]{:S(2)}) collective-permute-start(bf16[128,1536]{1,0:T(8,128)(2,1)S(1)} %get-tuple-element.23), channel_id=1, source_target_pairs={{0,2},{2,4},{4,6},{6,0},{64,70},{66,64},{68,66},{70,68},{1,3},{3,5... | collective-permute-start | bytes 1179656 | tf_op jit(solution)/shard_map/ppermute | solution.py:276
  46.8 0.9 dynamic_slice.10
  47.7 1.9 %collective-permute-start.2 = (bf16[64,1536]{1,0:T(8,128)(2,1)S(1)}, bf16[64,1536]{1,0:T(8,128)(2,1)S(1)}, u32[]{:S(2)}, u32[]{:S(2)}) collective-permute-start(bf16[64,1536]{1,0:T(8,128)(2,1)S(1)} %dynamic_slice.10), channel_id=1, source_target_pairs={{0,4},{2,6},{4,0},{6,2},{1,5},{3,7},{5,1},{7,3},{8,12},{10,14},{12... | collective-permute-start | bytes 589832 | tf_op jit(solution)/shard_map/ppermute | solution.py:252
  49.6 10.9 %all-to-all-done.1.refs_2_ = bf16[4,640,128]{2,1,0:T(8,128)(2,1)S(1)} async-done(((bf16[4,640,128]{2,1,0:T(8,128)(2,1)}), bf16[4,640,128]{2,1,0:T(8,128)(2,1)S(1)}, u32[]{:S(2)}, u32[]{:S(2)}) %all-to-all-start.1) | async-done | bytes 655392 | tf_op jit(solution)/shard_map/all_to_all | solution.py:267
  60.5 6.1 %attention.1 = bf16[8,336,128]{2,1,0:T(8,128)(2,1)} custom-call(bf16[8,320,128]{2,1,0:T(8,128)(2,1)S(1)} %all-to-all-done.refs_0_, bf16[4,640,128]{2,1,0:T(8,128)(2,1)S(1)} %bitcast.9, bf16[4,640,128]{2,1,0:T(8,128)(2,1)S(1)} %all-to-all-done.1.refs_2_), custom_call_target="tpu_custom_call" | custom-call | flops 2516582400 | bytes 4000000 | tf_op jit(solution)/shard_map/attention/pallas_call | solution.py:112
  66.6 0.8 collective-permute-done.2.refs_3_
  67.4 0.0 collective-permute-done.1.refs_2_
  67.4 4.4 %all-to-all-start.2 = ((bf16[8,336,128]{2,1,0:T(8,128)(2,1)}), bf16[8,336,128]{2,1,0:T(8,128)(2,1)S(1)}, u32[]{:S(2)}, u32[]{:S(2)}) async-start(bf16[8,336,128]{2,1,0:T(8,128)(2,1)} %attention.1), calls=%async_computation.2 | async-start | bytes 1376256 | tf_op jit(solution)/shard_map/all_to_all | solution.py:281
  71.8 0.1 stack.27.refs_0_
  71.9 0.6 cut_columns.1
  72.5 2.7 %collective-permute-start.3 = (bf16[320,768]{1,0:T(8,128)(2,1)S(1)}, bf16[320,768]{1,0:T(8,128)(2,1)S(1)}, u32[]{:S(2)}, u32[]{:S(2)}) collective-permute-start(bf16[320,768]{1,0:T(8,128)(2,1)S(1)} %get-tuple-element.21), channel_id=1, source_target_pairs={{0,1},{1,0},{2,3},{3,2},{4,5},{5,4},{6,7},{7,6},{8,9},{9,8},{10,11... | collective-permute-start | bytes 1474568 | tf_op jit(solution)/shard_map/ppermute | solution.py:252
  75.2 1.4 %collective-permute-done.3.refs_3_ = bf16[320,768]{1,0:T(8,128)(2,1)S(1)} collective-permute-done((bf16[320,768]{1,0:T(8,128)(2,1)S(1)}, bf16[320,768]{1,0:T(8,128)(2,1)S(1)}, u32[]{:S(2)}, u32[]{:S(2)}) %collective-permute-start.3) | collective-permute-done | bytes 491552 | tf_op jit(solution)/shard_map/ppermute | solution.py:252
  76.7 6.0 %collective-permute-start.4 = (bf16[384,768]{1,0:T(8,128)(2,1)S(1)}, bf16[384,768]{1,0:T(8,128)(2,1)S(1)}, u32[]{:S(2)}, u32[]{:S(2)}) collective-permute-start(bf16[384,768]{1,0:T(8,128)(2,1)S(1)} %pad_maximum_fusion), channel_id=1, source_target_pairs={{0,448},{64,128},{128,64},{192,256},{256,192},{320,384},{384,320},... | collective-permute-start | bytes 1769480 | tf_op jit(solution)/shard_map/ppermute | solution.py:287
  82.8 0.0 all-to-all-done.2.refs_0_
  82.8 0.7 merge.1
  83.5 17.0 %all-gather.1 = bf16[2560,128]{1,0:T(8,128)(2,1)S(1)} all-gather(bf16[320,128]{1,0:T(8,128)(2,1)S(1)} %merge.1), channel_id=3, replica_groups=mesh['zh'=4,'zl'=2,'yh'=2,'x'=4,'yl'=4,'c'=2] {'yl','c'}, dimensions={0}, use_global_device_ids=true | all-gather | bytes 737280 | tf_op jit(solution)/shard_map/all_gather | solution.py:288
  100.5 0.0 collective-permute-done.4.refs_4_
  100.5 2.1 %project.1 = (bf16[160,768]{1,0:T(8,128)(2,1)}, bf16[160,768]{1,0:T(8,128)(2,1)}) custom-call(s32[6]{0:T(128)S(1)} %stack.27.refs_0_, bf16[8,320,128]{2,1,0:T(8,128)(2,1)S(1)} %bitcast.8, bf16[320,768]{1,0:T(8,128)(2,1)S(1)} %get-tuple-element.20.refs_2_, bf16[320,768]{1,0:T(8,128)(2,1)S(1)} %collective-permute-done.3.refs_3_, ...), custom_call_target="tpu_custom_call" | custom-call | flops 503316480 | bytes 4000000 | tf_op jit(solution)/shard_map/project/pallas_call | solution.py:211
  (3 shorter events, 0.1 us)
Async XLA Ops:
  2.5 6.8 %copy-start = (bf16[640,128]{1,0:T(8,128)(2,1)S(1)}, bf16[640,128]{1,0:T(8,128)(2,1)}, u32[]{:S(2)}) copy-start(bf16[640,128]{1,0:T(8,128)(2,1)} %get-tuple-element.12) | copy-start | bytes 491524
  2.5 33.8 %all-to-all-start = ((bf16[8,320,128]{2,1,0:T(8,128)(2,1)}), bf16[8,320,128]{2,1,0:T(8,128)(2,1)S(1)}, u32[]{:S(2)}, u32[]{:S(2)}) async-start(bf16[8,320,128]{2,1,0:T(8,128)(2,1)} %get-tuple-element.13), calls=%async_computation | async-start | bytes 1310720 | tf_op jit(solution)/shard_map/all_to_all | solution.py:263
  9.3 27.0 %collective-permute-start = (bf16[640,128]{1,0:T(8,128)(2,1)S(1)}, bf16[640,128]{1,0:T(8,128)(2,1)S(1)}, u32[]{:S(2)}, u32[]{:S(2)}) collective-permute-start(bf16[640,128]{1,0:T(8,128)(2,1)S(1)} %copy-done), channel_id=1, source_target_pairs={{0,32},{32,0},{1,33},{33,1},{2,34},{34,2},{3,35},{35,3},{4,36},{36... | collective-permute-start | bytes 491528 | tf_op jit(solution)/shard_map/ppermute | solution.py:252
  37.2 23.3 %all-to-all-start.1 = ((bf16[4,640,128]{2,1,0:T(8,128)(2,1)}), bf16[4,640,128]{2,1,0:T(8,128)(2,1)S(1)}, u32[]{:S(2)}, u32[]{:S(2)}) async-start(bf16[4,640,128]{2,1,0:T(8,128)(2,1)} %broadcast_in_dim.2), calls=%async_computation.1 | async-start | bytes 1310720 | tf_op jit(solution)/shard_map/all_to_all | solution.py:267
  44.3 23.2 %collective-permute-start.1 = (bf16[128,1536]{1,0:T(8,128)(2,1)S(1)}, bf16[128,1536]{1,0:T(8,128)(2,1)S(1)}, u32[]{:S(2)}, u32[]{:S(2)}) collective-permute-start(bf16[128,1536]{1,0:T(8,128)(2,1)S(1)} %get-tuple-element.23), channel_id=1, source_target_pairs={{0,2},{2,4},{4,6},{6,0},{64,70},{66,64},{68,66},{70,68},{1,3},{3,5... | collective-permute-start | bytes 1179656 | tf_op jit(solution)/shard_map/ppermute | solution.py:276
  47.7 19.7 %collective-permute-start.2 = (bf16[64,1536]{1,0:T(8,128)(2,1)S(1)}, bf16[64,1536]{1,0:T(8,128)(2,1)S(1)}, u32[]{:S(2)}, u32[]{:S(2)}) collective-permute-start(bf16[64,1536]{1,0:T(8,128)(2,1)S(1)} %dynamic_slice.10), channel_id=1, source_target_pairs={{0,4},{2,6},{4,0},{6,2},{1,5},{3,7},{5,1},{7,3},{8,12},{10,14},{12... | collective-permute-start | bytes 589832 | tf_op jit(solution)/shard_map/ppermute | solution.py:252
  67.4 15.4 %all-to-all-start.2 = ((bf16[8,336,128]{2,1,0:T(8,128)(2,1)}), bf16[8,336,128]{2,1,0:T(8,128)(2,1)S(1)}, u32[]{:S(2)}, u32[]{:S(2)}) async-start(bf16[8,336,128]{2,1,0:T(8,128)(2,1)} %attention.1), calls=%async_computation.2 | async-start | bytes 1376256 | tf_op jit(solution)/shard_map/all_to_all | solution.py:281
  72.5 4.2 %collective-permute-start.3 = (bf16[320,768]{1,0:T(8,128)(2,1)S(1)}, bf16[320,768]{1,0:T(8,128)(2,1)S(1)}, u32[]{:S(2)}, u32[]{:S(2)}) collective-permute-start(bf16[320,768]{1,0:T(8,128)(2,1)S(1)} %get-tuple-element.21), channel_id=1, source_target_pairs={{0,1},{1,0},{2,3},{3,2},{4,5},{5,4},{6,7},{7,6},{8,9},{9,8},{10,11... | collective-permute-start | bytes 1474568 | tf_op jit(solution)/shard_map/ppermute | solution.py:252
  76.7 23.7 %collective-permute-start.4 = (bf16[384,768]{1,0:T(8,128)(2,1)S(1)}, bf16[384,768]{1,0:T(8,128)(2,1)S(1)}, u32[]{:S(2)}, u32[]{:S(2)}) collective-permute-start(bf16[384,768]{1,0:T(8,128)(2,1)S(1)} %pad_maximum_fusion), channel_id=1, source_target_pairs={{0,448},{64,128},{128,64},{192,256},{256,192},{320,384},{384,320},... | collective-permute-start | bytes 1769480 | tf_op jit(solution)/shard_map/ppermute | solution.py:287

commit v4 on v3

--- a/solution.py
+++ b/solution.py
@@ -92,7 +92,7 @@
     span_rows = step_blocks * rows
 
     def step(i, carry):
-        span = pl.ds(pl.multiple_of(i * span_rows, span_rows), span_rows)
+        span = pl.ds(i * span_rows, span_rows)
         mean, tangent, log, slope = attention_tile(qq, kk, vv, span)
         stats = three_parts(log) + three_parts(slope)
         for b in range(step_blocks):
@@ -103,10 +103,11 @@
             out_ref[at, 2 * rows:, :] = stat_rows([s[part] for s in stats], rows)
         return carry
 
-    lax.fori_loop(0, blocks // step_blocks, step, 0)
-
-
-def attention(queries, keys, rows, step_blocks=4):
+    for i in range(blocks // step_blocks):
+        step(i, 0)
+
+
+def attention(queries, keys, rows, step_blocks=2):
     blocks, nkeys = queries.shape[0], sum(p.shape[0] for p in keys) * rows
     work = blocks * rows * nkeys * HD
     return pl.pallas_call(
@@ -280,12 +281,14 @@
     partial, w_next, w_half = lax.optimization_barrier((partial, w_next, w_half))
     parts = lax.all_to_all(partial, ("x", "zl"), 0, 0, tiled=True)
     heads = [yl, yl - step, yl + step, yl + 2]
-    places = jnp.stack([core, zl] + [head % 4 for head in heads]).astype(jnp.int32)
+    heads = [head % 4 for head in heads]
+    places = jnp.stack([core, zl] + [head ^ (head >> 1) for head in heads]).astype(jnp.int32)
     keep, give = cut_columns(places, (w_own, w_next, w_half))
     got = turn(give, "c", 2, 1)
     near = [(z, (z + 1) % 8 if z % 2 else (z - 1) % 8) for z in range(8)]
     others = lax.ppermute(jnp.concatenate([keep[HD:], got[HD:]]), ("zh", "zl"), near)
-    attn = lax.all_gather(merge(parts, rows), ("yl", "c"), axis=0)
+    folded = [2 * y + c for y in (0, 1, 3, 2) for c in range(2)]
+    attn = lax.all_gather(merge(parts, rows), ("yl", "c"), axis_index_groups=[folded], axis=0)
     return project(places, attn, keep, got, others)
 
 

time: 103 us -> 102 us (level)
  blocking collectives: 36.5 us -> 34.8 us
    all_gather x1, blocking collectives: 17 us -> 15.4 us  [per_device(): lax.all_gather(merge(parts, rows), ('yl', 'c'), axis_index_groups=[folded...]
where the time goes in v4:
time: 102 us; the launch traced here: 101 us
  starting transfers between devices  37.7 us (37%)
  blocking collectives  34.8 us (34%)
  waiting for transfers between devices  13.5 us (13%)
  Pallas kernels  11 us (11%)
  local copies, waits for them, and re-layouts  3.17 us (3%)
    all_gather x1, blocking collectives, per_device(): k_first = lax.all_gather(k_own, 'zh', axis=0)  19.5 us
    all_gather x1, blocking collectives, per_device(): lax.all_gather(merge(parts, rows), ('yl', 'c'), axis_index_groups=[folded...  15.4 us
    ppermute x3, starting transfers between devices, turn(): lax.ppermute(array, axis, [(i, (i + offset) % count) for i in range(count)])  12.1 us
    all_to_all x1, waiting for transfers between devices, per_device(): k_second = lax.all_to_all(k_second, 'zh', 0, 0, tiled=True)  10.9 us
    all_to_all x1, starting transfers between devices, per_device(): q_all = lax.all_to_all(q_spread, ('x', 'zl'), 0, 0, tiled=True)  6.79 us
    ppermute x1, starting transfers between devices, per_device(): lax.ppermute(jnp.concatenate([keep[HD:], got[HD:]]), ('zh', 'zl'), near)  6.04 us
    all_to_all x1, starting transfers between devices, per_device(): k_second = lax.all_to_all(k_second, 'zh', 0, 0, tiled=True)  5.93 us
    pallas_call x1, Pallas kernels, attention(): pl.pallas_call(lambda *refs: attention_body(rows, step_blocks, *refs), ou...  5.77 us
  transfers between devices with their start and end apart: 8, of which 3 were waited for; matrix products, arithmetic and copies ran while one was open for 2% of the time, Pallas kernels for 7%

profile of v4, /device:TPU:1, one launch (start us, length us, event | category | flops | bytes accessed | tf_op | source)
XLA Modules:
  0.0 100.9 jit_solution(5365626840390842691)
XLA Ops:
  0.6 1.8 %prepare.1 = (bf16[8,320,128]{2,1,0:T(8,128)(2,1)}, bf16[640,128]{1,0:T(8,128)(2,1)}) custom-call(bf16[160,128]{1,0:T(8,128)(2,1)} %refs_0_.1, bf16[160,128]{1,0:T(8,128)(2,1)} %refs_1_.1, bf16[160,128]{1,0:T(8,128)(2,1)} %refs_2_.1, bf16[160,128]{1,0:T(8,128)(2,1)} %refs_3_.1, bf16[160,128]{1,0:T(8,128)(2,1)} %refs_4_.1, bf16[160,128]{1,0:T(8,128)(2,1)} %refs_5_.1), custom_call_target="tpu_custom_call" | custom-call | tf_op jit(solution)/shard_map/prepare/pallas_call | solution.py:238
  2.5 0.0 copy-start
  2.5 6.8 %all-to-all-start = ((bf16[8,320,128]{2,1,0:T(8,128)(2,1)}), bf16[8,320,128]{2,1,0:T(8,128)(2,1)S(1)}, u32[]{:S(2)}, u32[]{:S(2)}) async-start(bf16[8,320,128]{2,1,0:T(8,128)(2,1)} %get-tuple-element.13), calls=%async_computation | async-start | bytes 1310720 | tf_op jit(solution)/shard_map/all_to_all | solution.py:264
  9.3 0.0 copy-done
  9.3 7.5 %collective-permute-start = (bf16[640,128]{1,0:T(8,128)(2,1)S(1)}, bf16[640,128]{1,0:T(8,128)(2,1)S(1)}, u32[]{:S(2)}, u32[]{:S(2)}) collective-permute-start(bf16[640,128]{1,0:T(8,128)(2,1)S(1)} %copy-done), channel_id=1, source_target_pairs={{0,32},{32,0},{1,33},{33,1},{2,34},{34,2},{3,35},{35,3},{4,36},{36... | collective-permute-start | bytes 491528 | tf_op jit(solution)/shard_map/ppermute | solution.py:253
  16.7 19.5 %all-gather = bf16[2560,128]{1,0:T(8,128)(2,1)S(1)} all-gather(bf16[640,128]{1,0:T(8,128)(2,1)S(1)} %copy-done), channel_id=2, replica_groups=mesh['zh'=4,'zl'=2,'yh'=2,'x'=4,'yl'=4,'c'=2] {'zh'}, dimensions={0}, use_global_device_ids=true | all-gather | bytes 819200 | tf_op jit(solution)/shard_map/all_gather | solution.py:265
  36.2 0.0 collective-permute-done
  36.2 0.0 all-to-all-done.refs_0_
  36.2 0.9 broadcast_in_dim.2
  37.2 5.9 %all-to-all-start.1 = ((bf16[4,640,128]{2,1,0:T(8,128)(2,1)}), bf16[4,640,128]{2,1,0:T(8,128)(2,1)S(1)}, u32[]{:S(2)}, u32[]{:S(2)}) async-start(bf16[4,640,128]{2,1,0:T(8,128)(2,1)} %broadcast_in_dim.2), calls=%async_computation.1 | async-start | bytes 1310720 | tf_op jit(solution)/shard_map/all_to_all | solution.py:268
  43.1 1.2 %constant_dynamic-slice_fusion = (bf16[128,1536]{1,0:T(8,128)(2,1)S(1)}, bf16[128,1536]{1,0:T(8,128)(2,1)S(1)}) fusion(bf16[128,6144]{1,0:T(8,128)(2,1)} %param.13, s32[]{:T(128)S(6)} %select_n.49, s32[]{:T(128)S(6)} %select_n.46), kind=kLoop, calls=%fused_computation.1 | loop fusion | bytes 1572872 | tf_op jit(solution)/shard_map/dynamic_slice | solution.py:272
  44.3 2.5 %collective-permute-start.1 = (bf16[128,1536]{1,0:T(8,128)(2,1)S(1)}, bf16[128,1536]{1,0:T(8,128)(2,1)S(1)}, u32[]{:S(2)}, u32[]{:S(2)}) collective-permute-start(bf16[128,1536]{1,0:T(8,128)(2,1)S(1)} %get-tuple-element.23), channel_id=1, source_target_pairs={{0,2},{2,4},{4,6},{6,0},{64,70},{66,64},{68,66},{70,68},{1,3},{3,5... | collective-permute-start | bytes 1179656 | tf_op jit(solution)/shard_map/ppermute | solution.py:277
  46.8 0.9 dynamic_slice.10
  47.7 1.9 %collective-permute-start.2 = (bf16[64,1536]{1,0:T(8,128)(2,1)S(1)}, bf16[64,1536]{1,0:T(8,128)(2,1)S(1)}, u32[]{:S(2)}, u32[]{:S(2)}) collective-permute-start(bf16[64,1536]{1,0:T(8,128)(2,1)S(1)} %dynamic_slice.10), channel_id=1, source_target_pairs={{0,4},{2,6},{4,0},{6,2},{1,5},{3,7},{5,1},{7,3},{8,12},{10,14},{12... | collective-permute-start | bytes 589832 | tf_op jit(solution)/shard_map/ppermute | solution.py:253
  49.6 10.9 %all-to-all-done.1.refs_2_ = bf16[4,640,128]{2,1,0:T(8,128)(2,1)S(1)} async-done(((bf16[4,640,128]{2,1,0:T(8,128)(2,1)}), bf16[4,640,128]{2,1,0:T(8,128)(2,1)S(1)}, u32[]{:S(2)}, u32[]{:S(2)}) %all-to-all-start.1) | async-done | bytes 655392 | tf_op jit(solution)/shard_map/all_to_all | solution.py:268
  60.5 5.8 %attention.1 = bf16[8,336,128]{2,1,0:T(8,128)(2,1)} custom-call(bf16[8,320,128]{2,1,0:T(8,128)(2,1)S(1)} %all-to-all-done.refs_0_, bf16[4,640,128]{2,1,0:T(8,128)(2,1)S(1)} %bitcast.9, bf16[4,640,128]{2,1,0:T(8,128)(2,1)S(1)} %all-to-all-done.1.refs_2_), custom_call_target="tpu_custom_call" | custom-call | flops 2516582400 | bytes 4000000 | tf_op jit(solution)/shard_map/attention/pallas_call | solution.py:113
  66.3 1.1 %collective-permute-done.2.refs_3_ = bf16[64,1536]{1,0:T(8,128)(2,1)S(1)} collective-permute-done((bf16[64,1536]{1,0:T(8,128)(2,1)S(1)}, bf16[64,1536]{1,0:T(8,128)(2,1)S(1)}, u32[]{:S(2)}, u32[]{:S(2)}) %collective-permute-start.2) | collective-permute-done | bytes 196640 | tf_op jit(solution)/shard_map/ppermute | solution.py:253
  67.4 0.0 collective-permute-done.1.refs_2_
  67.4 4.4 %all-to-all-start.2 = ((bf16[8,336,128]{2,1,0:T(8,128)(2,1)}), bf16[8,336,128]{2,1,0:T(8,128)(2,1)S(1)}, u32[]{:S(2)}, u32[]{:S(2)}) async-start(bf16[8,336,128]{2,1,0:T(8,128)(2,1)} %attention.1), calls=%async_computation.2 | async-start | bytes 1376256 | tf_op jit(solution)/shard_map/all_to_all | solution.py:282
  71.8 0.1 stack.27.refs_0_
  71.9 0.6 cut_columns.1
  72.5 2.7 %collective-permute-start.3 = (bf16[320,768]{1,0:T(8,128)(2,1)S(1)}, bf16[320,768]{1,0:T(8,128)(2,1)S(1)}, u32[]{:S(2)}, u32[]{:S(2)}) collective-permute-start(bf16[320,768]{1,0:T(8,128)(2,1)S(1)} %get-tuple-element.21), channel_id=1, source_target_pairs={{0,1},{1,0},{2,3},{3,2},{4,5},{5,4},{6,7},{7,6},{8,9},{9,8},{10,11... | collective-permute-start | bytes 1474568 | tf_op jit(solution)/shard_map/ppermute | solution.py:253
  75.2 1.4 %collective-permute-done.3.refs_3_ = bf16[320,768]{1,0:T(8,128)(2,1)S(1)} collective-permute-done((bf16[320,768]{1,0:T(8,128)(2,1)S(1)}, bf16[320,768]{1,0:T(8,128)(2,1)S(1)}, u32[]{:S(2)}, u32[]{:S(2)}) %collective-permute-start.3) | collective-permute-done | bytes 491552 | tf_op jit(solution)/shard_map/ppermute | solution.py:253
  76.7 6.0 %collective-permute-start.4 = (bf16[384,768]{1,0:T(8,128)(2,1)S(1)}, bf16[384,768]{1,0:T(8,128)(2,1)S(1)}, u32[]{:S(2)}, u32[]{:S(2)}) collective-permute-start(bf16[384,768]{1,0:T(8,128)(2,1)S(1)} %pad_maximum_fusion), channel_id=1, source_target_pairs={{0,448},{64,128},{128,64},{192,256},{256,192},{320,384},{384,320},... | collective-permute-start | bytes 1769480 | tf_op jit(solution)/shard_map/ppermute | solution.py:289
  82.8 0.0 all-to-all-done.2.refs_0_
  82.8 0.7 merge.1
  83.5 15.4 %all-gather.1 = bf16[2560,128]{1,0:T(8,128)(2,1)S(1)} all-gather(bf16[320,128]{1,0:T(8,128)(2,1)S(1)} %merge.1), channel_id=3, replica_groups={{0,1,2,3,6,7,4,5},{8,9,10,11,14,15,12,13},{16,17,18,19,22,23,20,21},{24..., dimensions={0}, use_global_device_ids=true | all-gather | bytes 737280 | tf_op jit(solution)/shard_map/all_gather | solution.py:291
  98.9 0.0 collective-permute-done.4.refs_4_
  98.9 2.1 %project.1 = (bf16[160,768]{1,0:T(8,128)(2,1)}, bf16[160,768]{1,0:T(8,128)(2,1)}) custom-call(s32[6]{0:T(128)S(1)} %stack.27.refs_0_, bf16[8,320,128]{2,1,0:T(8,128)(2,1)S(1)} %bitcast.8, bf16[320,768]{1,0:T(8,128)(2,1)S(1)} %get-tuple-element.20.refs_2_, bf16[320,768]{1,0:T(8,128)(2,1)S(1)} %collective-permute-done.3.refs_3_, ...), custom_call_target="tpu_custom_call" | custom-call | flops 503316480 | bytes 4000000 | tf_op jit(solution)/shard_map/project/pallas_call | solution.py:212
  (3 shorter events, 0.1 us)
Async XLA Ops:
  2.5 6.8 %copy-start = (bf16[640,128]{1,0:T(8,128)(2,1)S(1)}, bf16[640,128]{1,0:T(8,128)(2,1)}, u32[]{:S(2)}) copy-start(bf16[640,128]{1,0:T(8,128)(2,1)} %get-tuple-element.12) | copy-start | bytes 491524
  2.5 33.8 %all-to-all-start = ((bf16[8,320,128]{2,1,0:T(8,128)(2,1)}), bf16[8,320,128]{2,1,0:T(8,128)(2,1)S(1)}, u32[]{:S(2)}, u32[]{:S(2)}) async-start(bf16[8,320,128]{2,1,0:T(8,128)(2,1)} %get-tuple-element.13), calls=%async_computation | async-start | bytes 1310720 | tf_op jit(solution)/shard_map/all_to_all | solution.py:264
  9.3 27.0 %collective-permute-start = (bf16[640,128]{1,0:T(8,128)(2,1)S(1)}, bf16[640,128]{1,0:T(8,128)(2,1)S(1)}, u32[]{:S(2)}, u32[]{:S(2)}) collective-permute-start(bf16[640,128]{1,0:T(8,128)(2,1)S(1)} %copy-done), channel_id=1, source_target_pairs={{0,32},{32,0},{1,33},{33,1},{2,34},{34,2},{3,35},{35,3},{4,36},{36... | collective-permute-start | bytes 491528 | tf_op jit(solution)/shard_map/ppermute | solution.py:253
  37.2 23.3 %all-to-all-start.1 = ((bf16[4,640,128]{2,1,0:T(8,128)(2,1)}), bf16[4,640,128]{2,1,0:T(8,128)(2,1)S(1)}, u32[]{:S(2)}, u32[]{:S(2)}) async-start(bf16[4,640,128]{2,1,0:T(8,128)(2,1)} %broadcast_in_dim.2), calls=%async_computation.1 | async-start | bytes 1310720 | tf_op jit(solution)/shard_map/all_to_all | solution.py:268
  44.3 23.2 %collective-permute-start.1 = (bf16[128,1536]{1,0:T(8,128)(2,1)S(1)}, bf16[128,1536]{1,0:T(8,128)(2,1)S(1)}, u32[]{:S(2)}, u32[]{:S(2)}) collective-permute-start(bf16[128,1536]{1,0:T(8,128)(2,1)S(1)} %get-tuple-element.23), channel_id=1, source_target_pairs={{0,2},{2,4},{4,6},{6,0},{64,70},{66,64},{68,66},{70,68},{1,3},{3,5... | collective-permute-start | bytes 1179656 | tf_op jit(solution)/shard_map/ppermute | solution.py:277
  47.7 19.7 %collective-permute-start.2 = (bf16[64,1536]{1,0:T(8,128)(2,1)S(1)}, bf16[64,1536]{1,0:T(8,128)(2,1)S(1)}, u32[]{:S(2)}, u32[]{:S(2)}) collective-permute-start(bf16[64,1536]{1,0:T(8,128)(2,1)S(1)} %dynamic_slice.10), channel_id=1, source_target_pairs={{0,4},{2,6},{4,0},{6,2},{1,5},{3,7},{5,1},{7,3},{8,12},{10,14},{12... | collective-permute-start | bytes 589832 | tf_op jit(solution)/shard_map/ppermute | solution.py:253
  67.4 15.4 %all-to-all-start.2 = ((bf16[8,336,128]{2,1,0:T(8,128)(2,1)}), bf16[8,336,128]{2,1,0:T(8,128)(2,1)S(1)}, u32[]{:S(2)}, u32[]{:S(2)}) async-start(bf16[8,336,128]{2,1,0:T(8,128)(2,1)} %attention.1), calls=%async_computation.2 | async-start | bytes 1376256 | tf_op jit(solution)/shard_map/all_to_all | solution.py:282
  72.5 4.2 %collective-permute-start.3 = (bf16[320,768]{1,0:T(8,128)(2,1)S(1)}, bf16[320,768]{1,0:T(8,128)(2,1)S(1)}, u32[]{:S(2)}, u32[]{:S(2)}) collective-permute-start(bf16[320,768]{1,0:T(8,128)(2,1)S(1)} %get-tuple-element.21), channel_id=1, source_target_pairs={{0,1},{1,0},{2,3},{3,2},{4,5},{5,4},{6,7},{7,6},{8,9},{9,8},{10,11... | collective-permute-start | bytes 1474568 | tf_op jit(solution)/shard_map/ppermute | solution.py:253
  76.7 22.1 %collective-permute-start.4 = (bf16[384,768]{1,0:T(8,128)(2,1)S(1)}, bf16[384,768]{1,0:T(8,128)(2,1)S(1)}, u32[]{:S(2)}, u32[]{:S(2)}) collective-permute-start(bf16[384,768]{1,0:T(8,128)(2,1)S(1)} %pad_maximum_fusion), channel_id=1, source_target_pairs={{0,448},{64,128},{128,64},{192,256},{256,192},{320,384},{384,320},... | collective-permute-start | bytes 1769480 | tf_op jit(solution)/shard_map/ppermute | solution.py:289

commit v5 on v4

--- a/solution.py
+++ b/solution.py
@@ -189,18 +189,20 @@
 
 def project_body(rows, at_ref, attn_ref, keep_ref, got_ref, others_ref, out_ref, tan_ref, left, right):
     core, half, part = at_ref[0], at_ref[1], HD // 2
+    total = jnp.zeros((2 * rows, keep_ref.shape[1]), F32)
     for c, ref in enumerate((keep_ref, got_ref)):
         first, theirs = 4 * c, (HD + part) * c
         for n in range(4):
             head = 2 * at_ref[2 + n] + (core if c == 0 else 1 - core)
             left[:, (first + n) * HD:(first + n + 1) * HD] = attn_ref[head]
-        base = first * HD
-        right[base:base + 2 * HD, :] = ref[:2 * HD, :]
-        right[base + 2 * HD:base + 3 * HD, :] = others_ref[theirs:theirs + HD, :]
-        low = base + 3 * HD
+        base = 2 * HD * c
+        right[base:base + HD, :] = others_ref[theirs:theirs + HD, :]
+        low = base + HD
         right[pl.ds(pl.multiple_of(low + half * part, part), part), :] = ref[2 * HD:, :]
         right[pl.ds(pl.multiple_of(low + (1 - half) * part, part), part), :] = others_ref[theirs + HD:theirs + HD + part, :]
-    total = dot_nn(left[...], right[...])
+        at = first * HD
+        total += dot_nn(left[:, at:at + 2 * HD], ref[:2 * HD, :])
+        total += dot_nn(left[:, at + 2 * HD:at + 4 * HD], right[base:base + 2 * HD, :])
     out_ref[...] = total[:rows].astype(BF16)
     tan_ref[...] = total[rows:].astype(BF16)
 
@@ -216,7 +218,7 @@
         out_specs=(WHOLE, WHOLE),
         scratch_shapes=[
             pltpu.VMEM((both, heads * HD), BF16),
-            pltpu.VMEM((heads * HD, columns), BF16),
+            pltpu.VMEM((heads // 2 * HD, columns), BF16),
         ],
         compiler_params=limit(12),
         cost_estimate=pl.CostEstimate(flops=2 * both * heads * HD * columns, bytes_accessed=4000000, transcendentals=0),

time: 102 us -> 101 us (level)
  no operation moved by 1% of the time
where the time goes in v5:
time: 101 us
  starting transfers between devices  37.7 us (37%)
  blocking collectives  34.8 us (34%)
  waiting for transfers between devices  13.5 us (13%)
  Pallas kernels  10.9 us (11%)
  local copies, waits for them, and re-layouts  3.17 us (3%)
    all_gather x1, blocking collectives, per_device(): k_first = lax.all_gather(k_own, 'zh', axis=0)  19.5 us
    all_gather x1, blocking collectives, per_device(): lax.all_gather(merge(parts, rows), ('yl', 'c'), axis_index_groups=[folded...  15.4 us
    ppermute x3, starting transfers between devices, turn(): lax.ppermute(array, axis, [(i, (i + offset) % count) for i in range(count)])  12.1 us
    all_to_all x1, waiting for transfers between devices, per_device(): k_second = lax.all_to_all(k_second, 'zh', 0, 0, tiled=True)  10.9 us
    all_to_all x1, starting transfers between devices, per_device(): q_all = lax.all_to_all(q_spread, ('x', 'zl'), 0, 0, tiled=True)  6.79 us
    ppermute x1, starting transfers between devices, per_device(): lax.ppermute(jnp.concatenate([keep[HD:], got[HD:]]), ('zh', 'zl'), near)  6.04 us
    all_to_all x1, starting transfers between devices, per_device(): k_second = lax.all_to_all(k_second, 'zh', 0, 0, tiled=True)  5.93 us
    pallas_call x1, Pallas kernels, attention(): pl.pallas_call(lambda *refs: attention_body(rows, step_blocks, *refs), ou...  5.77 us
  transfers between devices with their start and end apart: 8, of which 3 were waited for; matrix products, arithmetic and copies ran while one was open for 2% of the time, Pallas kernels for 7%

profile of v5, /device:TPU:1, one launch (start us, length us, event | category | flops | bytes accessed | tf_op | source)
XLA Modules:
  0.0 100.8 jit_solution(17801950644008831814)
XLA Ops:
  0.6 1.8 %prepare.1 = (bf16[8,320,128]{2,1,0:T(8,128)(2,1)}, bf16[640,128]{1,0:T(8,128)(2,1)}) custom-call(bf16[160,128]{1,0:T(8,128)(2,1)} %refs_0_.1, bf16[160,128]{1,0:T(8,128)(2,1)} %refs_1_.1, bf16[160,128]{1,0:T(8,128)(2,1)} %refs_2_.1, bf16[160,128]{1,0:T(8,128)(2,1)} %refs_3_.1, bf16[160,128]{1,0:T(8,128)(2,1)} %refs_4_.1, bf16[160,128]{1,0:T(8,128)(2,1)} %refs_5_.1), custom_call_target="tpu_custom_call" | custom-call | tf_op jit(solution)/shard_map/prepare/pallas_call | solution.py:240
  2.5 0.0 copy-start
  2.5 6.8 %all-to-all-start = ((bf16[8,320,128]{2,1,0:T(8,128)(2,1)}), bf16[8,320,128]{2,1,0:T(8,128)(2,1)S(1)}, u32[]{:S(2)}, u32[]{:S(2)}) async-start(bf16[8,320,128]{2,1,0:T(8,128)(2,1)} %get-tuple-element.13), calls=%async_computation | async-start | bytes 1310720 | tf_op jit(solution)/shard_map/all_to_all | solution.py:266
  9.3 0.0 copy-done
  9.3 7.5 %collective-permute-start = (bf16[640,128]{1,0:T(8,128)(2,1)S(1)}, bf16[640,128]{1,0:T(8,128)(2,1)S(1)}, u32[]{:S(2)}, u32[]{:S(2)}) collective-permute-start(bf16[640,128]{1,0:T(8,128)(2,1)S(1)} %copy-done), channel_id=1, source_target_pairs={{0,32},{32,0},{1,33},{33,1},{2,34},{34,2},{3,35},{35,3},{4,36},{36... | collective-permute-start | bytes 491528 | tf_op jit(solution)/shard_map/ppermute | solution.py:255
  16.7 19.5 %all-gather = bf16[2560,128]{1,0:T(8,128)(2,1)S(1)} all-gather(bf16[640,128]{1,0:T(8,128)(2,1)S(1)} %copy-done), channel_id=2, replica_groups=mesh['zh'=4,'zl'=2,'yh'=2,'x'=4,'yl'=4,'c'=2] {'zh'}, dimensions={0}, use_global_device_ids=true | all-gather | bytes 819200 | tf_op jit(solution)/shard_map/all_gather | solution.py:267
  36.2 0.0 collective-permute-done
  36.2 0.0 all-to-all-done.refs_0_
  36.2 0.9 broadcast_in_dim.2
  37.2 5.9 %all-to-all-start.1 = ((bf16[4,640,128]{2,1,0:T(8,128)(2,1)}), bf16[4,640,128]{2,1,0:T(8,128)(2,1)S(1)}, u32[]{:S(2)}, u32[]{:S(2)}) async-start(bf16[4,640,128]{2,1,0:T(8,128)(2,1)} %broadcast_in_dim.2), calls=%async_computation.1 | async-start | bytes 1310720 | tf_op jit(solution)/shard_map/all_to_all | solution.py:270
  43.1 1.2 %constant_dynamic-slice_fusion = (bf16[128,1536]{1,0:T(8,128)(2,1)S(1)}, bf16[128,1536]{1,0:T(8,128)(2,1)S(1)}) fusion(bf16[128,6144]{1,0:T(8,128)(2,1)} %param.13, s32[]{:T(128)S(6)} %select_n.49, s32[]{:T(128)S(6)} %select_n.46), kind=kLoop, calls=%fused_computation.1 | loop fusion | bytes 1572872 | tf_op jit(solution)/shard_map/dynamic_slice | solution.py:274
  44.3 2.5 %collective-permute-start.1 = (bf16[128,1536]{1,0:T(8,128)(2,1)S(1)}, bf16[128,1536]{1,0:T(8,128)(2,1)S(1)}, u32[]{:S(2)}, u32[]{:S(2)}) collective-permute-start(bf16[128,1536]{1,0:T(8,128)(2,1)S(1)} %get-tuple-element.23), channel_id=1, source_target_pairs={{0,2},{2,4},{4,6},{6,0},{64,70},{66,64},{68,66},{70,68},{1,3},{3,5... | collective-permute-start | bytes 1179656 | tf_op jit(solution)/shard_map/ppermute | solution.py:279
  46.8 0.9 dynamic_slice.10
  47.7 1.9 %collective-permute-start.2 = (bf16[64,1536]{1,0:T(8,128)(2,1)S(1)}, bf16[64,1536]{1,0:T(8,128)(2,1)S(1)}, u32[]{:S(2)}, u32[]{:S(2)}) collective-permute-start(bf16[64,1536]{1,0:T(8,128)(2,1)S(1)} %dynamic_slice.10), channel_id=1, source_target_pairs={{0,4},{2,6},{4,0},{6,2},{1,5},{3,7},{5,1},{7,3},{8,12},{10,14},{12... | collective-permute-start | bytes 589832 | tf_op jit(solution)/shard_map/ppermute | solution.py:255
  49.6 10.9 %all-to-all-done.1.refs_2_ = bf16[4,640,128]{2,1,0:T(8,128)(2,1)S(1)} async-done(((bf16[4,640,128]{2,1,0:T(8,128)(2,1)}), bf16[4,640,128]{2,1,0:T(8,128)(2,1)S(1)}, u32[]{:S(2)}, u32[]{:S(2)}) %all-to-all-start.1) | async-done | bytes 655392 | tf_op jit(solution)/shard_map/all_to_all | solution.py:270
  60.5 5.8 %attention.1 = bf16[8,336,128]{2,1,0:T(8,128)(2,1)} custom-call(bf16[8,320,128]{2,1,0:T(8,128)(2,1)S(1)} %all-to-all-done.refs_0_, bf16[4,640,128]{2,1,0:T(8,128)(2,1)S(1)} %bitcast.9, bf16[4,640,128]{2,1,0:T(8,128)(2,1)S(1)} %all-to-all-done.1.refs_2_), custom_call_target="tpu_custom_call" | custom-call | flops 2516582400 | bytes 4000000 | tf_op jit(solution)/shard_map/attention/pallas_call | solution.py:113
  66.3 1.1 %collective-permute-done.2.refs_3_ = bf16[64,1536]{1,0:T(8,128)(2,1)S(1)} collective-permute-done((bf16[64,1536]{1,0:T(8,128)(2,1)S(1)}, bf16[64,1536]{1,0:T(8,128)(2,1)S(1)}, u32[]{:S(2)}, u32[]{:S(2)}) %collective-permute-start.2) | collective-permute-done | bytes 196640 | tf_op jit(solution)/shard_map/ppermute | solution.py:255
  67.4 0.0 collective-permute-done.1.refs_2_
  67.4 4.4 %all-to-all-start.2 = ((bf16[8,336,128]{2,1,0:T(8,128)(2,1)}), bf16[8,336,128]{2,1,0:T(8,128)(2,1)S(1)}, u32[]{:S(2)}, u32[]{:S(2)}) async-start(bf16[8,336,128]{2,1,0:T(8,128)(2,1)} %attention.1), calls=%async_computation.2 | async-start | bytes 1376256 | tf_op jit(solution)/shard_map/all_to_all | solution.py:284
  71.8 0.1 stack.27.refs_0_
  71.9 0.6 cut_columns.1
  72.5 2.7 %collective-permute-start.3 = (bf16[320,768]{1,0:T(8,128)(2,1)S(1)}, bf16[320,768]{1,0:T(8,128)(2,1)S(1)}, u32[]{:S(2)}, u32[]{:S(2)}) collective-permute-start(bf16[320,768]{1,0:T(8,128)(2,1)S(1)} %get-tuple-element.21), channel_id=1, source_target_pairs={{0,1},{1,0},{2,3},{3,2},{4,5},{5,4},{6,7},{7,6},{8,9},{9,8},{10,11... | collective-permute-start | bytes 1474568 | tf_op jit(solution)/shard_map/ppermute | solution.py:255
  75.2 1.4 %collective-permute-done.3.refs_3_ = bf16[320,768]{1,0:T(8,128)(2,1)S(1)} collective-permute-done((bf16[320,768]{1,0:T(8,128)(2,1)S(1)}, bf16[320,768]{1,0:T(8,128)(2,1)S(1)}, u32[]{:S(2)}, u32[]{:S(2)}) %collective-permute-start.3) | collective-permute-done | bytes 491552 | tf_op jit(solution)/shard_map/ppermute | solution.py:255
  76.7 6.0 %collective-permute-start.4 = (bf16[384,768]{1,0:T(8,128)(2,1)S(1)}, bf16[384,768]{1,0:T(8,128)(2,1)S(1)}, u32[]{:S(2)}, u32[]{:S(2)}) collective-permute-start(bf16[384,768]{1,0:T(8,128)(2,1)S(1)} %pad_maximum_fusion), channel_id=1, source_target_pairs={{0,448},{64,128},{128,64},{192,256},{256,192},{320,384},{384,320},... | collective-permute-start | bytes 1769480 | tf_op jit(solution)/shard_map/ppermute | solution.py:291
  82.8 0.0 all-to-all-done.2.refs_0_
  82.8 0.7 merge.1
  83.5 15.4 %all-gather.1 = bf16[2560,128]{1,0:T(8,128)(2,1)S(1)} all-gather(bf16[320,128]{1,0:T(8,128)(2,1)S(1)} %merge.1), channel_id=3, replica_groups={{0,1,2,3,6,7,4,5},{8,9,10,11,14,15,12,13},{16,17,18,19,22,23,20,21},{24..., dimensions={0}, use_global_device_ids=true | all-gather | bytes 737280 | tf_op jit(solution)/shard_map/all_gather | solution.py:293
  98.9 0.0 collective-permute-done.4.refs_4_
  98.9 2.0 %project.1 = (bf16[160,768]{1,0:T(8,128)(2,1)}, bf16[160,768]{1,0:T(8,128)(2,1)}) custom-call(s32[6]{0:T(128)S(1)} %stack.27.refs_0_, bf16[8,320,128]{2,1,0:T(8,128)(2,1)S(1)} %bitcast.8, bf16[320,768]{1,0:T(8,128)(2,1)S(1)} %get-tuple-element.20.refs_2_, bf16[320,768]{1,0:T(8,128)(2,1)S(1)} %collective-permute-done.3.refs_3_, ...), custom_call_target="tpu_custom_call" | custom-call | flops 503316480 | bytes 4000000 | tf_op jit(solution)/shard_map/project/pallas_call | solution.py:214
  (3 shorter events, 0.1 us)
Async XLA Ops:
  2.5 6.8 %copy-start = (bf16[640,128]{1,0:T(8,128)(2,1)S(1)}, bf16[640,128]{1,0:T(8,128)(2,1)}, u32[]{:S(2)}) copy-start(bf16[640,128]{1,0:T(8,128)(2,1)} %get-tuple-element.12) | copy-start | bytes 491524
  2.5 33.8 %all-to-all-start = ((bf16[8,320,128]{2,1,0:T(8,128)(2,1)}), bf16[8,320,128]{2,1,0:T(8,128)(2,1)S(1)}, u32[]{:S(2)}, u32[]{:S(2)}) async-start(bf16[8,320,128]{2,1,0:T(8,128)(2,1)} %get-tuple-element.13), calls=%async_computation | async-start | bytes 1310720 | tf_op jit(solution)/shard_map/all_to_all | solution.py:266
  9.3 27.0 %collective-permute-start = (bf16[640,128]{1,0:T(8,128)(2,1)S(1)}, bf16[640,128]{1,0:T(8,128)(2,1)S(1)}, u32[]{:S(2)}, u32[]{:S(2)}) collective-permute-start(bf16[640,128]{1,0:T(8,128)(2,1)S(1)} %copy-done), channel_id=1, source_target_pairs={{0,32},{32,0},{1,33},{33,1},{2,34},{34,2},{3,35},{35,3},{4,36},{36... | collective-permute-start | bytes 491528 | tf_op jit(solution)/shard_map/ppermute | solution.py:255
  37.2 23.3 %all-to-all-start.1 = ((bf16[4,640,128]{2,1,0:T(8,128)(2,1)}), bf16[4,640,128]{2,1,0:T(8,128)(2,1)S(1)}, u32[]{:S(2)}, u32[]{:S(2)}) async-start(bf16[4,640,128]{2,1,0:T(8,128)(2,1)} %broadcast_in_dim.2), calls=%async_computation.1 | async-start | bytes 1310720 | tf_op jit(solution)/shard_map/all_to_all | solution.py:270
  44.3 23.2 %collective-permute-start.1 = (bf16[128,1536]{1,0:T(8,128)(2,1)S(1)}, bf16[128,1536]{1,0:T(8,128)(2,1)S(1)}, u32[]{:S(2)}, u32[]{:S(2)}) collective-permute-start(bf16[128,1536]{1,0:T(8,128)(2,1)S(1)} %get-tuple-element.23), channel_id=1, source_target_pairs={{0,2},{2,4},{4,6},{6,0},{64,70},{66,64},{68,66},{70,68},{1,3},{3,5... | collective-permute-start | bytes 1179656 | tf_op jit(solution)/shard_map/ppermute | solution.py:279
  47.7 19.7 %collective-permute-start.2 = (bf16[64,1536]{1,0:T(8,128)(2,1)S(1)}, bf16[64,1536]{1,0:T(8,128)(2,1)S(1)}, u32[]{:S(2)}, u32[]{:S(2)}) collective-permute-start(bf16[64,1536]{1,0:T(8,128)(2,1)S(1)} %dynamic_slice.10), channel_id=1, source_target_pairs={{0,4},{2,6},{4,0},{6,2},{1,5},{3,7},{5,1},{7,3},{8,12},{10,14},{12... | collective-permute-start | bytes 589832 | tf_op jit(solution)/shard_map/ppermute | solution.py:255
  67.4 15.4 %all-to-all-start.2 = ((bf16[8,336,128]{2,1,0:T(8,128)(2,1)}), bf16[8,336,128]{2,1,0:T(8,128)(2,1)S(1)}, u32[]{:S(2)}, u32[]{:S(2)}) async-start(bf16[8,336,128]{2,1,0:T(8,128)(2,1)} %attention.1), calls=%async_computation.2 | async-start | bytes 1376256 | tf_op jit(solution)/shard_map/all_to_all | solution.py:284
  72.5 4.2 %collective-permute-start.3 = (bf16[320,768]{1,0:T(8,128)(2,1)S(1)}, bf16[320,768]{1,0:T(8,128)(2,1)S(1)}, u32[]{:S(2)}, u32[]{:S(2)}) collective-permute-start(bf16[320,768]{1,0:T(8,128)(2,1)S(1)} %get-tuple-element.21), channel_id=1, source_target_pairs={{0,1},{1,0},{2,3},{3,2},{4,5},{5,4},{6,7},{7,6},{8,9},{9,8},{10,11... | collective-permute-start | bytes 1474568 | tf_op jit(solution)/shard_map/ppermute | solution.py:255
  76.7 22.1 %collective-permute-start.4 = (bf16[384,768]{1,0:T(8,128)(2,1)S(1)}, bf16[384,768]{1,0:T(8,128)(2,1)S(1)}, u32[]{:S(2)}, u32[]{:S(2)}) collective-permute-start(bf16[384,768]{1,0:T(8,128)(2,1)S(1)} %pad_maximum_fusion), channel_id=1, source_target_pairs={{0,448},{64,128},{128,64},{192,256},{256,192},{320,384},{384,320},... | collective-permute-start | bytes 1769480 | tf_op jit(solution)/shard_map/ppermute | solution.py:291
